TPU v7x, 32 devices: a whole 2x2x4 slice. The times are simulated.
32 devices in a mesh: dp: 8 (over z, y), chan: 4 (over x, core).
Axes of the slice: x: 2, y: 2, z: 4, core: 2. Of those that a mesh axis runs over, the one named last changes fastest.
Arguments:
- latents: bfloat16 [16, 576, 1536], P('dp', None, 'chan'), may hold values from -6 to 6
- valid_mask: int32 [16, 576], P('dp'), may hold values from 0 to 1, as said below
- bucket_ids: int32 [16], P('dp'), may hold values from 0 to 2
- text_count: int32 [16], P('dp'), may hold values from 19 to 77, as said below
- text_tokens: bfloat16 [16, 77, 1536], P('dp', None, 'chan'), may hold values from -6 to 6
- noise_embed: float32 [16, 64], P('dp'), may hold values from -5 to 5
- conv_kernel: float32 [9, 1536], P(None, 'chan'), may hold values from -2 to 2
- conv_bias: float32 [1536], P('chan'), may hold values from -2 to 2
- mixer_expand_weight: bfloat16 [1536, 6144], P(None, 'chan'), may hold values from -0.15625 to 0.15625
- ffn_in_bias: float32 [6144], P('chan'), may hold values from -2 to 2
- grn_gamma: float32 [6144], P('chan'), may hold values from -4 to 4
- grn_beta: float32 [6144], P('chan'), may hold values from -2 to 2
- mixer_contract_weight: bfloat16 [6144, 1536], P('chan'), may hold values from -0.078125 to 0.078125
- ffn_out_bias: float32 [1536], P('chan'), may hold values from -2 to 2
- scale_weight: float32 [64, 1536], P(None, 'chan'), may hold values from -0.1875 to 0.1875
- scale_bias: float32 [1536], P('chan'), may hold values from -1 to 1
- shift_weight: float32 [64, 1536], P(None, 'chan'), may hold values from -0.375 to 0.375
- shift_bias: float32 [1536], P('chan'), may hold values from -2 to 2
- text_weight: bfloat16 [1536, 1536], P(None, 'chan'), may hold values from -0.15625 to 0.15625
- text_bias: float32 [1536], P('chan'), may hold values from -2 to 2
- query_weight: bfloat16 [1536, 1536], P(None, 'chan'), may hold values from -0.15625 to 0.15625
- query_bias: float32 [1536], P('chan'), may hold values from -2 to 2
- key_weight: bfloat16 [1536, 1536], P(None, 'chan'), may hold values from -0.15625 to 0.15625
- value_weight: bfloat16 [1536, 1536], P(None, 'chan'), may hold values from -0.15625 to 0.15625
- value_bias: float32 [1536], P('chan'), may hold values from -2 to 2
- attn_out: bfloat16 [1536, 1536], P('chan'), may hold values from -0.625 to 0.625
- attn_out_bias: float32 [1536], P('chan'), may hold values from -2 to 2
- upstream: bfloat16 [16, 576, 1536], P('dp', None, 'chan'), may hold values from -6 to 6
Outputs:
- result: bfloat16 [16, 576, 1536], P('dp', None, 'chan')
- grad_latents: bfloat16 [16, 576, 1536], P('dp', None, 'chan')
- grad_conv_kernel: float32 [9, 1536], P(None, 'chan')
- grad_conv_bias: float32 [1536], P('chan')
- grad_ffn_in: float32 [1536, 6144], P('dp', 'chan')
- grad_ffn_in_bias: float32 [6144], P('chan')
- grad_grn_gamma: float32 [6144], P('chan')
- grad_grn_beta: float32 [6144], P('chan')
- mixer_contract_gradient: float32 [6144, 1536], P('chan', 'dp')
- grad_ffn_out_bias: float32 [1536], P('chan')
- grad_scale_weight: float32 [64, 1536], P(None, 'chan')
- grad_scale_bias: float32 [1536], P('chan')
- grad_shift_weight: float32 [64, 1536], P(None, 'chan')
- grad_shift_bias: float32 [1536], P('chan')
- grad_text_weight: float32 [1536, 1536], P('dp', 'chan')
- grad_text_bias: float32 [1536], P('chan')
- grad_query_weight: float32 [1536, 1536], P('dp', 'chan')
- grad_query_bias: float32 [1536], P('chan')
- grad_key_weight: float32 [1536, 1536], P('dp', 'chan')
- grad_value_weight: float32 [1536, 1536], P('dp', 'chan')
- grad_value_bias: float32 [1536], P('chan')
- grad_attn_out: float32 [1536, 1536], P('chan', 'dp')
- grad_attn_out_bias: float32 [1536], P('chan')
Inputs may be any that keep to these rules, and one draw needn't show every extreme that they name: `valid_mask`: A latent's valid slots are its first ones in slot order, at least 558 of them; some latent has all valid and some has exactly that least number. `text_count`: some latent has all 77 text tokens valid and some has 19.
All inputs are finite; a program needn't handle non-finite values.
Results may differ from a plain program's by a relative error of at most 0.02.
Values may be sent and summed in bfloat16 or wider, within the bound.
No kernel may reach another device: no remote copies, remote signals or barrier semaphores. Data moves between devices by JAX's collectives and lax.ppermute only.
A program may use at most 256 MiB of HBM per device.

v0:
```python
import jax
import jax.numpy as jnp
from jax import lax
from jax.sharding import PartitionSpec as P

C = 1536
HEADS = 24


def depthwise_one(masked, widths, heights, kernel, kernel_bias):
    slot_count = masked.shape[0]
    places = jnp.arange(slot_count, dtype=jnp.int32)
    row_pos = places // widths
    col_pos = places % widths
    margin = 40
    padded = jnp.pad(masked, ((margin, margin), (0, 0)))
    summed = jnp.zeros_like(masked) + kernel_bias
    for row_step in (-1, 0, 1):
        for col_step in (-1, 0, 1):
            offset = margin + row_step * widths + col_step
            shifted = lax.dynamic_slice_in_dim(padded, offset, slot_count, 0)
            inside = (
                (row_pos + row_step >= 0)
                & (row_pos + row_step < heights)
                & (col_pos + col_step >= 0)
                & (col_pos + col_step < widths)
            )
            summed = (
                summed
                + jnp.where(inside[:, None], shifted, 0.0)
                * kernel[(row_step + 1) * 3 + col_step + 1]
            )
    return summed


def channel_stats(parts):
    return lax.psum(parts, "chan")


def gather_rows(values):
    return lax.all_gather(values, "chan", axis=2, tiled=True)


def scatter_rows(values):
    return lax.psum_scatter(
        values.astype(jnp.bfloat16), "chan", scatter_dimension=2, tiled=True
    ).astype(jnp.float32)


def norm_forward(values, width_total):
    sums = channel_stats((jnp.sum(values, axis=-1), jnp.sum(values * values, axis=-1)))
    mean_value = sums[0] / width_total
    variance = sums[1] / width_total - mean_value * mean_value
    inverse = lax.rsqrt(variance + 1e-06)
    return ((values - mean_value[..., None]) * inverse[..., None], inverse)


def norm_backward(grad_norm, normed, inverse, width_total):
    sums = channel_stats((jnp.sum(grad_norm, axis=-1), jnp.sum(grad_norm * normed, axis=-1)))
    mean_grad = sums[0][..., None] / width_total
    mean_cross = sums[1][..., None] / width_total
    return inverse[..., None] * (grad_norm - mean_grad - normed * mean_cross)


def gelu_exact(values):
    return jax.nn.gelu(values, approximate=False)


def local(
    latents,
    valid_mask,
    bucket_ids,
    text_count,
    text_tokens,
    noise_embed,
    conv_kernel,
    conv_bias,
    mixer_expand_weight,
    ffn_in_bias,
    grn_gamma,
    grn_beta,
    mixer_contract_weight,
    ffn_out_bias,
    scale_weight,
    scale_bias,
    shift_weight,
    shift_bias,
    text_weight,
    text_bias,
    query_weight,
    query_bias,
    key_weight,
    value_weight,
    value_bias,
    attn_out,
    attn_out_bias,
    upstream,
):
    lat_count, slot_count, chan_local = latents.shape
    chan_total = chan_local * lax.axis_size("chan")
    hidden_total = mixer_expand_weight.shape[1] * lax.axis_size("chan")
    head_dim = C // HEADS
    head_local = chan_local // head_dim
    text_len = text_tokens.shape[1]
    key_rows = slot_count + text_len
    factor = head_dim ** (-0.5)
    highest = lax.Precision.HIGHEST
    mask_float = valid_mask.astype(jnp.float32)[..., None]
    widths = jnp.where(bucket_ids == 0, 36, jnp.where(bucket_ids == 1, 24, 18)).astype(jnp.int32)
    heights = jnp.where(bucket_ids == 0, 16, jnp.where(bucket_ids == 1, 24, 32)).astype(jnp.int32)
    inputs_f = latents.astype(jnp.float32)

    def conv_apply(masked_in, kernel, kernel_bias):
        return jax.vmap(depthwise_one, in_axes=(0, 0, 0, None, None))(
            masked_in, widths, heights, kernel, kernel_bias
        )

    conv_out, conv_pullback = jax.vjp(conv_apply, inputs_f * mask_float, conv_kernel, conv_bias)
    normed_one, inverse_one = norm_forward(conv_out, chan_total)
    gathered_single = gather_rows(normed_one.astype(jnp.bfloat16))
    hidden_pre = (
        jnp.einsum(
            "mvd,dx->mvx", gathered_single, mixer_expand_weight, preferred_element_type=jnp.float32
        )
        + ffn_in_bias
    )
    active, gelu_pullback = jax.vjp(gelu_exact, hidden_pre)
    spatial = jnp.sqrt(jnp.sum(mask_float * active * active, axis=1))
    spatial_total = channel_stats((jnp.sum(spatial, axis=-1),))[0]
    denom = spatial_total / hidden_total + 1e-06
    response = spatial / denom[:, None]
    gated_reduced = (grn_gamma * (active * response[:, None, :]) + grn_beta + active).astype(
        jnp.bfloat16
    )
    branch = (
        scatter_rows(
            jnp.einsum(
                "jvn,nr->jvr",
                gated_reduced,
                mixer_contract_weight,
                preferred_element_type=jnp.float32,
            )
        )
        + ffn_out_bias
    )
    first = inputs_f + branch
    scale_rows = jnp.dot(noise_embed, scale_weight, precision=highest) + scale_bias
    shift_rows = jnp.dot(noise_embed, shift_weight, precision=highest) + shift_bias
    second = first * (1.0 + scale_rows[:, None, :]) + shift_rows[:, None, :]
    normed_two, inverse_two = norm_forward(second, chan_total)
    text_act = jax.nn.silu(text_tokens.astype(jnp.float32)).astype(jnp.bfloat16)
    text_full = lax.all_gather(text_act, "chan", axis=2, tiled=True)
    text_low = (
        jnp.einsum("ltc,cd->ltd", text_full, text_weight, preferred_element_type=jnp.float32)
        + text_bias
    ).astype(jnp.bfloat16)
    context_full = gather_rows(jnp.concatenate([normed_two.astype(jnp.bfloat16), text_low], axis=1))
    slot_context = context_full[:, :slot_count]
    queries = (
        jnp.einsum("lsc,cd->lsd", slot_context, query_weight, preferred_element_type=jnp.float32)
        + query_bias
    ).astype(jnp.bfloat16)
    keys = jnp.einsum(
        "lsc,cd->lsd", context_full, key_weight, preferred_element_type=jnp.float32
    ).astype(jnp.bfloat16)
    values = (
        jnp.einsum("lsc,cd->lsd", context_full, value_weight, preferred_element_type=jnp.float32)
        + value_bias
    ).astype(jnp.bfloat16)
    head_q = queries.reshape(lat_count, slot_count, head_local, head_dim)
    head_k = keys.reshape(lat_count, key_rows, head_local, head_dim)
    head_v = values.reshape(lat_count, key_rows, head_local, head_dim)
    text_valid = jnp.arange(text_len, dtype=jnp.int32)[None, :] < text_count[:, None]
    key_valid = jnp.concatenate([valid_mask > 0, text_valid], axis=1)

    def scores_of():
        raw = (
            jnp.einsum("lqhd,lkhd->lhqk", head_q, head_k, preferred_element_type=jnp.float32)
            * factor
        )
        return jnp.where(key_valid[:, None, None, :], raw, -1e30)

    scores = scores_of()
    top_score = jnp.max(scores, axis=-1, keepdims=True)
    expo = jnp.exp(scores - top_score)
    weight_total = jnp.sum(expo, axis=-1, keepdims=True)
    probs = expo / weight_total
    log_total = top_score + jnp.log(weight_total)
    attended = jnp.einsum(
        "lhqk,lkhd->lqhd", probs.astype(jnp.bfloat16), head_v, preferred_element_type=jnp.float32
    )
    attended_low = attended.astype(jnp.bfloat16).reshape(lat_count, slot_count, chan_local)
    branch_two = (
        scatter_rows(
            jnp.einsum("lsc,cd->lsd", attended_low, attn_out, preferred_element_type=jnp.float32)
        )
        + attn_out_bias
    )
    result = (second + branch_two).astype(jnp.bfloat16)
    grad_out = upstream.astype(jnp.float32)
    grad_attn_out_bias = jnp.sum(grad_out, axis=(0, 1))
    grad_full = gather_rows(upstream)
    grad_attn_out = jnp.einsum(
        "lsc,lsd->cd", attended_low, grad_full, preferred_element_type=jnp.float32
    )
    grad_attended = jnp.einsum(
        "lsd,cd->lsc", grad_full, attn_out, preferred_element_type=jnp.float32
    ).astype(jnp.bfloat16)
    grad_attended = grad_attended.reshape(lat_count, slot_count, head_local, head_dim)
    probs_back = jnp.exp(scores_of() - log_total)
    grad_probs = jnp.einsum(
        "lqhd,lkhd->lhqk", grad_attended, head_v, preferred_element_type=jnp.float32
    )
    grad_values = jnp.einsum(
        "lhqk,lqhd->lkhd",
        probs_back.astype(jnp.bfloat16),
        grad_attended,
        preferred_element_type=jnp.float32,
    ).astype(jnp.bfloat16)
    row_dot = jnp.sum(probs_back * grad_probs, axis=-1, keepdims=True)
    grad_scores = (probs_back * (grad_probs - row_dot)).astype(jnp.bfloat16)
    grad_queries = (
        jnp.einsum("lhqk,lkhd->lqhd", grad_scores, head_k, preferred_element_type=jnp.float32)
        * factor
    ).astype(jnp.bfloat16)
    grad_keys = (
        jnp.einsum("lhqk,lqhd->lkhd", grad_scores, head_q, preferred_element_type=jnp.float32)
        * factor
    ).astype(jnp.bfloat16)
    grad_queries = grad_queries.reshape(lat_count, slot_count, chan_local)
    grad_keys = grad_keys.reshape(lat_count, key_rows, chan_local)
    grad_values = grad_values.reshape(lat_count, key_rows, chan_local)
    grad_query_bias = jnp.sum(grad_queries.astype(jnp.float32), axis=(0, 1))
    grad_value_bias = jnp.sum(grad_values.astype(jnp.float32), axis=(0, 1))
    grad_query_weight = jnp.einsum(
        "lsc,lsd->cd", slot_context, grad_queries, preferred_element_type=jnp.float32
    )
    grad_key_weight = jnp.einsum(
        "lsc,lsd->cd", context_full, grad_keys, preferred_element_type=jnp.float32
    )
    grad_value_weight = jnp.einsum(
        "lsc,lsd->cd", context_full, grad_values, preferred_element_type=jnp.float32
    )
    query_part = jnp.einsum(
        "lsd,cd->lsc", grad_queries, query_weight, preferred_element_type=jnp.float32
    )
    context_part = jnp.einsum(
        "lsd,cd->lsc", grad_keys, key_weight, preferred_element_type=jnp.float32
    )
    context_part = context_part + jnp.einsum(
        "lsd,cd->lsc", grad_values, value_weight, preferred_element_type=jnp.float32
    )
    context_part = context_part + jnp.pad(query_part, ((0, 0), (0, text_len), (0, 0)))
    grad_context = scatter_rows(context_part)
    grad_text_low = grad_context[:, slot_count:].astype(jnp.bfloat16)
    grad_text_bias = jnp.sum(grad_text_low.astype(jnp.float32), axis=(0, 1))
    grad_text_weight = jnp.einsum(
        "ltc,ltd->cd", text_full, grad_text_low, preferred_element_type=jnp.float32
    )
    grad_second = grad_out + norm_backward(
        grad_context[:, :slot_count], normed_two, inverse_two, chan_total
    )
    grad_scale_rows = jnp.sum(grad_second * first, axis=1)
    grad_shift_rows = jnp.sum(grad_second, axis=1)
    grad_scale_weight = jnp.dot(noise_embed.T, grad_scale_rows, precision=highest)
    grad_shift_weight = jnp.dot(noise_embed.T, grad_shift_rows, precision=highest)
    grad_scale_bias = jnp.sum(grad_scale_rows, axis=0)
    grad_shift_bias = jnp.sum(grad_shift_rows, axis=0)
    grad_first = grad_second * (1.0 + scale_rows[:, None, :])
    grad_ffn_out_bias = jnp.sum(grad_first, axis=(0, 1))
    branch_gradient_total = gather_rows(grad_first.astype(jnp.bfloat16))
    mixer_contract_gradient = jnp.einsum(
        "irz,irk->zk", gated_reduced, branch_gradient_total, preferred_element_type=jnp.float32
    )
    grad_gated = jnp.einsum(
        "dxw,nw->dxn",
        branch_gradient_total,
        mixer_contract_weight,
        preferred_element_type=jnp.float32,
    )
    active_back, gelu_back = (active, gelu_pullback)
    grad_grn_gamma = jnp.sum(grad_gated * active_back * response[:, None, :], axis=(0, 1))
    grad_grn_beta = jnp.sum(grad_gated, axis=(0, 1))
    grad_response = jnp.sum(grad_gated * grn_gamma * active_back, axis=1)
    grad_active = grad_gated * (grn_gamma * response[:, None, :] + 1.0)
    cross_total = channel_stats((jnp.sum(grad_response * spatial, axis=-1),))[0]
    grad_spatial = (
        grad_response / denom[:, None] - (cross_total / (denom * denom))[:, None] / hidden_total
    )
    grad_active = grad_active + (grad_spatial / spatial)[:, None, :] * mask_float * active_back
    hidden_gradient = gelu_back(grad_active)[0].astype(jnp.bfloat16)
    grad_ffn_in_bias = jnp.sum(hidden_gradient.astype(jnp.float32), axis=(0, 1))
    grad_ffn_in = jnp.einsum(
        "noe,noi->ei", gathered_single, hidden_gradient, preferred_element_type=jnp.float32
    )
    grad_normed_one = scatter_rows(
        jnp.einsum(
            "biw,ow->bio", hidden_gradient, mixer_expand_weight, preferred_element_type=jnp.float32
        )
    )
    grad_conv_out = norm_backward(grad_normed_one, normed_one, inverse_one, chan_total)
    grad_masked, grad_conv_kernel, grad_conv_bias = conv_pullback(grad_conv_out)
    grad_latents = (grad_first + grad_masked * mask_float).astype(jnp.bfloat16)
    (
        grad_ffn_in,
        mixer_contract_gradient,
        grad_query_weight,
        grad_key_weight,
        grad_value_weight,
        grad_text_weight,
        grad_attn_out,
    ) = (
        lax.psum_scatter(grad_ffn_in, "dp", scatter_dimension=0, tiled=True),
        lax.psum_scatter(mixer_contract_gradient, "dp", scatter_dimension=1, tiled=True),
        lax.psum_scatter(grad_query_weight, "dp", scatter_dimension=0, tiled=True),
        lax.psum_scatter(grad_key_weight, "dp", scatter_dimension=0, tiled=True),
        lax.psum_scatter(grad_value_weight, "dp", scatter_dimension=0, tiled=True),
        lax.psum_scatter(grad_text_weight, "dp", scatter_dimension=0, tiled=True),
        lax.psum_scatter(grad_attn_out, "dp", scatter_dimension=1, tiled=True),
    )
    summed_small = lax.psum(
        (
            grad_conv_kernel,
            grad_conv_bias,
            grad_ffn_in_bias,
            grad_grn_gamma,
            grad_grn_beta,
            grad_ffn_out_bias,
            grad_scale_weight,
            grad_scale_bias,
            grad_shift_weight,
            grad_shift_bias,
            grad_text_bias,
            grad_query_bias,
            grad_value_bias,
            grad_attn_out_bias,
        ),
        "dp",
    )
    return (
        result,
        grad_latents,
        summed_small[0],
        summed_small[1],
        grad_ffn_in,
        summed_small[2],
        summed_small[3],
        summed_small[4],
        mixer_contract_gradient,
        summed_small[5],
        summed_small[6],
        summed_small[7],
        summed_small[8],
        summed_small[9],
        grad_text_weight,
        summed_small[10],
        grad_query_weight,
        summed_small[11],
        grad_key_weight,
        grad_value_weight,
        summed_small[12],
        grad_attn_out,
        summed_small[13],
    )


def solution(mesh):
    in_specs = (
        P("dp", None, "chan"),
        P("dp", None),
        P("dp"),
        P("dp"),
        P("dp", None, "chan"),
        P("dp", None),
        P(None, "chan"),
        P("chan"),
        P(None, "chan"),
        P("chan"),
        P("chan"),
        P("chan"),
        P("chan", None),
        P("chan"),
        P(None, "chan"),
        P("chan"),
        P(None, "chan"),
        P("chan"),
        P(None, "chan"),
        P("chan"),
        P(None, "chan"),
        P("chan"),
        P(None, "chan"),
        P(None, "chan"),
        P("chan"),
        P("chan", None),
        P("chan"),
        P("dp", None, "chan"),
    )
    out_specs = (
        P("dp", None, "chan"),
        P("dp", None, "chan"),
        P(None, "chan"),
        P("chan"),
        P("dp", "chan"),
        P("chan"),
        P("chan"),
        P("chan"),
        P("chan", "dp"),
        P("chan"),
        P(None, "chan"),
        P("chan"),
        P(None, "chan"),
        P("chan"),
        P("dp", "chan"),
        P("chan"),
        P("dp", "chan"),
        P("chan"),
        P("dp", "chan"),
        P("dp", "chan"),
        P("chan"),
        P("chan", "dp"),
        P("chan"),
    )
    return jax.shard_map(local, mesh=mesh, in_specs=in_specs, out_specs=out_specs, check_vma=False)
```

profile of v0, /device:TPU:0, one launch (start us, length us, event | category | flops | bytes accessed | tf_op | source)
XLA Modules:
  0.0 1465.4 jit_solution(296921611466637232)
XLA Ops:
  14.2 5.8 while.26
  21.5 5.8 while.25
  35.9 5.8 while.23
  43.0 5.8 while.22
  50.2 5.8 while.21
  57.4 5.8 while.20
  64.6 5.9 while.19
  72.5 5.8 while.18
  79.5 6.8 fusion.91
  86.4 12.7 all-reduce.22
  100.6 31.1 %all-gather.5.cloned.1.call-done = bf16[2,576,1536]{2,1,0:T(8,128)(2,1)} async-done(((bf16[2,576,384]{2,1,0:T(8,128)(2,1)}), bf16[2,576,1536]{2,1,0:T(8,128)(2,1)}) %all-gather.5.cloned.1.call-update) | async-done | bytes 3538960 | tf_op jit(solution)/shard_map/all_gather | solution.py:41
  131.7 11.1 fusion.42
  142.9 18.6 %fusion.8 = (f32[2,1536]{1,0:T(2,128)S(1)}, f32[2,576,1536]{2,1,0:T(8,128)}, f32[2,576,1536]{2,1,0:T(8,128)}) fusion(f32[2,576]{1,0:T(2,128)S(1)} %convert_element_type.126, f32[2,576,1536]{2,1,0:T(8,128)S(1)} %get-tuple-element.638, f32[1536]{0:T(1024)S(1)} %copy-done.69, u8[576,1536]{1,0:T(8,128)(4,1)S(1)} %get-tuple-element.314, ...), kind=kLoop, calls=%fused_computation.63 | loop fusion | flops 129168384 | bytes 23026176 | tf_op jit(solution)/shard_map/reduce_sum | solution.py:128
  161.7 6.4 psum.170
  169.4 10.5 fusion.25
  179.9 10.6 copy.138
  190.4 8.7 reshape.1866
  200.1 7.1 all_gather.16
  208.5 32.2 %reduce-scatter.34.cloned.1.call-done = bf16[384,1152]{1,0:T(8,128)(2,1)} async-done(((bf16[1536,1152]{1,0:T(8,128)(2,1)}), bf16[384,1152]{1,0:T(8,128)(2,1)}) %reduce-scatter.34.cloned.1.call-update) | async-done | bytes 884752
  248.4 11.0 all-reduce.21
  261.3 12.1 all-gather.9.cloned.1.call-done
  279.1 29.9 %all-gather.7.cloned.1.call-done = bf16[2,653,1536]{2,1,0:T(8,128)(2,1)} async-done(((bf16[2,653,384]{2,1,0:T(8,128)(2,1)}), bf16[2,653,1536]{2,1,0:T(8,128)(2,1)}) %all-gather.7.cloned.1.call-update) | async-done | bytes 4012048 | tf_op jit(solution)/shard_map/all_gather | solution.py:41
  322.5 9.8 fusion.6
  332.3 12.2 fusion
  352.8 9.6 fusion.47
  367.3 10.6 copy.140
  377.9 9.1 reshape.1868
  387.1 14.6 multiply_reduce_fusion
  401.7 14.8 %multiply_convert_fusion = bf16[2,6,576,653]{2,3,1,0:T(8,128)(2,1)S(1)} fusion(f32[2,6,576,653]{2,3,1,0:T(8,128)} %get-tuple-element.642, f32[2,6,576]{2,1,0:T(8,128)S(1)} %get-tuple-element.641, f32[2,6,576]{2,1,0:T(8,128)S(1)} %copy-done.33, f32[2,6,576,653]{2,3,1,0:T(8,128)} %get-tuple-element.640, pred[2,653]{1,0:T(4,128)(4,1)S(1)} %pad_add_fusion.1), kind=kLoop, calls=%fused_computation.45 | loop fusion | flops 27081216 | bytes 45191960 | tf_op jit(solution)/shard_map/convert_element_type | solution.py:221
  426.4 6.9 fusion.54
  433.3 13.4 convert_reduce_fusion.3
  446.7 8.5 add_convert_fusion
  455.2 12.4 copy.142
  467.6 10.5 reshape.1870
  483.9 39.9 %reduce-scatter.38.cloned.1.call-done = bf16[384,1306]{1,0:T(8,128)(2,1)} async-done(((bf16[1536,1306]{1,0:T(8,128)(2,1)}), bf16[384,1306]{1,0:T(8,128)(2,1)}) %reduce-scatter.38.cloned.1.call-update) | async-done | bytes 1003024
  534.7 10.1 all-reduce.20
  552.1 31.8 %all-gather.11.cloned.1.call-done = bf16[2,576,1536]{2,1,0:T(8,128)(2,1)} async-done(((bf16[2,576,384]{2,1,0:T(8,128)(2,1)}), bf16[2,576,1536]{2,1,0:T(8,128)(2,1)}) %all-gather.11.cloned.1.call-update) | async-done | bytes 3538960 | tf_op jit(solution)/shard_map/all_gather | solution.py:41
  583.9 12.5 multiply_reduce_fusion.1
  596.6 5.9 psum.175
  602.6 11.5 convert_reduce_fusion
  615.9 9.4 fusion.22
  625.3 10.6 copy.144
  635.9 8.6 reshape.1872
  652.7 7.1 convolution_bitcast_fusion.3
  661.1 6.2 convolution_bitcast_fusion.2
  680.6 11.6 convolution_bitcast_fusion.1
  692.9 12.5 convolution_bitcast_fusion
  714.7 11.1 all-reduce.19
  729.5 8.2 fusion.90
  737.9 5.9 multiply_select_fusion.4
  744.5 22.5 %while.27 = (s32[]{:T(128)}, f32[2,656,384]{2,1,0:T(8,128)S(1)}, s32[2,3]{1,0:T(2,128)S(1)}, f32[2,576,384]{2,1,0:T(8,128)}, s32[]{:T(128)}, /*index=5*/s32[3]{0:T(128)S(1)}, s32[]{:T(128)}) while((s32[]{:T(128)}, f32[2,656,384]{2,1,0:T(8,128)S(1)}, s32[2,3]{1,0:T(2,128)S(1)}, f32[2,576,384]{2,1,0:T(8,128)}, s32[]{:T(128)}, ...), condition=%wide.while_cond.9, body=%wide.while_body.9.sunk | while | flops 442387 | bytes 4423859 | solution.py:21
  769.0 22.8 %while.28 = (s32[]{:T(128)}, f32[2,656,384]{2,1,0:T(8,128)}, s32[2,3]{1,0:T(2,128)S(1)}, f32[2,576,384]{2,1,0:T(8,128)}, s32[]{:T(128)}, /*index=5*/s32[3]{0:T(128)S(1)}, s32[]{:T(128)}) while((s32[]{:T(128)}, f32[2,656,384]{2,1,0:T(8,128)}, s32[2,3]{1,0:T(2,128)S(1)}, f32[2,576,384]{2,1,0:T(8,128)}, s32[]{:T(128)}, /*index=5*/s32[3]{0:T(128)S(1)}, ...), condition=%wide.while_cond.10, body=%wide.while_body.10.sunk | while | flops 442387 | bytes 4423859 | solution.py:21
  794.2 22.5 %while.29 = (s32[]{:T(128)}, f32[2,656,384]{2,1,0:T(8,128)S(1)}, s32[2,3]{1,0:T(2,128)S(1)}, f32[2,576,384]{2,1,0:T(8,128)}, s32[]{:T(128)}, /*index=5*/s32[3]{0:T(128)S(1)}, s32[]{:T(128)}) while((s32[]{:T(128)}, f32[2,656,384]{2,1,0:T(8,128)S(1)}, s32[2,3]{1,0:T(2,128)S(1)}, f32[2,576,384]{2,1,0:T(8,128)}, s32[]{:T(128)}, ...), condition=%wide.while_cond.11, body=%wide.while_body.11.sunk | while | flops 442387 | bytes 4423859 | solution.py:21
  818.2 22.9 %while.30 = (s32[]{:T(128)}, f32[2,656,384]{2,1,0:T(8,128)}, s32[2,3]{1,0:T(2,128)S(1)}, f32[2,576,384]{2,1,0:T(8,128)}, s32[]{:T(128)}, /*index=5*/s32[3]{0:T(128)S(1)}, s32[]{:T(128)}) while((s32[]{:T(128)}, f32[2,656,384]{2,1,0:T(8,128)}, s32[2,3]{1,0:T(2,128)S(1)}, f32[2,576,384]{2,1,0:T(8,128)}, s32[]{:T(128)}, /*index=5*/s32[3]{0:T(128)S(1)}, ...), condition=%wide.while_cond.12, body=%wide.while_body.12.sunk | while | flops 442387 | bytes 4423859 | solution.py:21
  844.2 22.9 %while.31 = (s32[]{:T(128)}, f32[2,656,384]{2,1,0:T(8,128)}, s32[2,3]{1,0:T(2,128)S(1)}, f32[2,576,384]{2,1,0:T(8,128)}, s32[]{:T(128)}, /*index=5*/s32[3]{0:T(128)S(1)}, s32[]{:T(128)}) while((s32[]{:T(128)}, f32[2,656,384]{2,1,0:T(8,128)}, s32[2,3]{1,0:T(2,128)S(1)}, f32[2,576,384]{2,1,0:T(8,128)}, s32[]{:T(128)}, /*index=5*/s32[3]{0:T(128)S(1)}, ...), condition=%wide.while_cond.13, body=%wide.while_body.13.sunk | while | flops 442387 | bytes 4423859 | solution.py:21
  868.5 23.0 %while.32 = (s32[]{:T(128)}, f32[2,656,384]{2,1,0:T(8,128)}, s32[2,3]{1,0:T(2,128)S(1)}, f32[2,576,384]{2,1,0:T(8,128)}, s32[]{:T(128)}, /*index=5*/s32[3]{0:T(128)S(1)}, s32[]{:T(128)}) while((s32[]{:T(128)}, f32[2,656,384]{2,1,0:T(8,128)}, s32[2,3]{1,0:T(2,128)S(1)}, f32[2,576,384]{2,1,0:T(8,128)}, s32[]{:T(128)}, /*index=5*/s32[3]{0:T(128)S(1)}, ...), condition=%wide.while_cond.14, body=%wide.while_body.14.sunk | while | flops 442387 | bytes 4423859 | solution.py:21
  894.5 22.9 %while.33 = (s32[]{:T(128)}, f32[2,656,384]{2,1,0:T(8,128)}, s32[2,3]{1,0:T(2,128)S(1)}, f32[2,576,384]{2,1,0:T(8,128)}, s32[]{:T(128)}, /*index=5*/s32[3]{0:T(128)S(1)}, s32[]{:T(128)}) while((s32[]{:T(128)}, f32[2,656,384]{2,1,0:T(8,128)}, s32[2,3]{1,0:T(2,128)S(1)}, f32[2,576,384]{2,1,0:T(8,128)}, s32[]{:T(128)}, /*index=5*/s32[3]{0:T(128)S(1)}, ...), condition=%wide.while_cond.15, body=%wide.while_body.15.sunk | while | flops 442387 | bytes 4423859 | solution.py:21
  918.9 23.1 %while.34 = (s32[]{:T(128)}, f32[2,656,384]{2,1,0:T(8,128)}, s32[2,3]{1,0:T(2,128)S(1)}, f32[2,576,384]{2,1,0:T(8,128)}, s32[]{:T(128)}, /*index=5*/s32[3]{0:T(128)S(1)}, s32[]{:T(128)}) while((s32[]{:T(128)}, f32[2,656,384]{2,1,0:T(8,128)}, s32[2,3]{1,0:T(2,128)S(1)}, f32[2,576,384]{2,1,0:T(8,128)}, s32[]{:T(128)}, /*index=5*/s32[3]{0:T(128)S(1)}, ...), condition=%wide.while_cond.16, body=%wide.while_body.16.sunk | while | flops 442387 | bytes 4423859 | solution.py:21
  945.1 39.0 %all-reduce.17 = (f32[9,384]{1,0:T(8,128)}, f32[384]{0:T(512)}, f32[1536]{0:T(1024)}, f32[1536]{0:T(1024)}, f32[1536]{0:T(1024)}, /*index=5*/f32[384]{0:T(512)},...) all-reduce(f32[9,384]{1,0:T(8,128)S(1)} %pad_add_fusion, ...), channel_id=1, replica_groups=mesh['dp'=8,'chan'=4] {'dp'}, use_global_device_ids=true, to_apply=%region_47.48 | all-reduce | flops 11136 | bytes 89088 | tf_op jit(solution)/shard_map/psum | solution.py:321
  984.1 22.7 %while.35 = (s32[]{:T(128)}, f32[2,656,384]{2,1,0:T(8,128)}, s32[2,3]{1,0:T(2,128)S(1)}, f32[2,576,384]{2,1,0:T(8,128)}, s32[]{:T(128)}, /*index=5*/s32[3]{0:T(128)S(1)}, s32[]{:T(128)}) while((s32[]{:T(128)}, f32[2,656,384]{2,1,0:T(8,128)}, s32[2,3]{1,0:T(2,128)S(1)}, f32[2,576,384]{2,1,0:T(8,128)}, s32[]{:T(128)}, /*index=5*/s32[3]{0:T(128)S(1)}, ...), condition=%wide.while_cond.17, body=%wide.while_body.17.sunk | while | flops 442387 | bytes 4423859 | solution.py:21
  1009.5 39.4 %all-reduce.25.cloned.1.call-done = (f32[64,384]{1,0:T(8,128)}, f32[64,384]{1,0:T(8,128)}) async-done(((f32[64,384]{1,0:T(8,128)}, f32[64,384]{1,0:T(8,128)}), (f32[64,384]{1,0:T(8,128)}, f32[64,384]{1,0:T(8,128)})) %all-reduce.25.cloned.1.call-update) | async-done | bytes 196624 | tf_op jit(solution)/shard_map/psum | solution.py:321
  1049.0 72.6 %reduce-scatter.24.cloned.1.call-done = f32[192,384]{1,0:T(8,128)} async-done(((f32[1536,384]{1,0:T(8,128)}), f32[192,384]{1,0:T(8,128)}) %reduce-scatter.24.cloned.1.call-update) | async-done | bytes 294928 | tf_op jit(solution)/shard_map/reduce_scatter | solution.py:318
  1121.5 167.0 %reduce-scatter.20.cloned.1.call-done = f32[192,1536]{1,0:T(8,128)} async-done(((f32[1536,1536]{1,0:T(8,128)}), f32[192,1536]{1,0:T(8,128)}) %reduce-scatter.20.cloned.1.call-update) | async-done | bytes 1179664 | tf_op jit(solution)/shard_map/reduce_scatter | solution.py:313
  1288.5 167.1 %reduce-scatter.22.cloned.1.call-done = f32[1536,192]{0,1:T(8,128)} async-done(((f32[1536,1536]{0,1:T(8,128)}), f32[1536,192]{0,1:T(8,128)}) %reduce-scatter.22.cloned.1.call-update) | async-done | bytes 1179664 | tf_op jit(solution)/shard_map/reduce_scatter | solution.py:314
  (564 shorter events, 425.6 us)
Async XLA Ops:
  7.2 301.8 %copy-start = (bf16[1536,384]{1,0:T(8,128)(2,1)S(1)}, bf16[1536,384]{1,0:T(8,128)(2,1)}, u32[]{:S(2)}) copy-start(bf16[1536,384]{1,0:T(8,128)(2,1)} %param.50) | copy-start | bytes 3538948
  7.2 124.5 %all-gather.5.cloned.1.call-start = ((), (), s32[]{:S(2)}) async-start(), calls=%async_computation.11 | async-start | bytes 4423680 | tf_op jit(solution)/shard_map/all_gather | solution.py:41
  8.0 134.9 %copy-start.39 = (f32[2,576]{1,0:T(2,128)}, f32[2,576]{1,0:T(2,128)S(1)}, u32[]{:S(2)}) copy-start(f32[2,576]{1,0:T(2,128)S(1)} %convert_element_type.126) | copy-start | bytes 13828
  9.1 70.2 %copy-start.76 = (f32[384]{0:T(512)}, f32[384]{0:T(512)S(1)}, u32[]{:S(2)}) copy-start(f32[384]{0:T(512)S(1)} %get-tuple-element.339) | copy-start | bytes 4612
  9.1 70.2 %copy-start.78 = (f32[384]{0:T(512)}, f32[384]{0:T(512)S(1)}, u32[]{:S(2)}) copy-start(f32[384]{0:T(512)S(1)} %get-tuple-element.340) | copy-start | bytes 4612
  9.1 70.2 %copy-start.80 = (f32[384]{0:T(512)}, f32[384]{0:T(512)S(1)}, u32[]{:S(2)}) copy-start(f32[384]{0:T(512)S(1)} %get-tuple-element.341) | copy-start | bytes 4612
  9.1 70.2 %copy-start.82 = (f32[384]{0:T(512)}, f32[384]{0:T(512)S(1)}, u32[]{:S(2)}) copy-start(f32[384]{0:T(512)S(1)} %get-tuple-element.342) | copy-start | bytes 4612
  9.1 70.2 %copy-start.84 = (f32[384]{0:T(512)}, f32[384]{0:T(512)S(1)}, u32[]{:S(2)}) copy-start(f32[384]{0:T(512)S(1)} %get-tuple-element.343) | copy-start | bytes 4612
  9.1 70.2 %copy-start.86 = (f32[384]{0:T(512)}, f32[384]{0:T(512)S(1)}, u32[]{:S(2)}) copy-start(f32[384]{0:T(512)S(1)} %get-tuple-element.344) | copy-start | bytes 4612
  9.2 70.2 %copy-start.88 = (f32[384]{0:T(512)}, f32[384]{0:T(512)S(1)}, u32[]{:S(2)}) copy-start(f32[384]{0:T(512)S(1)} %get-tuple-element.345) | copy-start | bytes 4612
  9.2 70.2 %copy-start.90 = (f32[384]{0:T(512)}, f32[384]{0:T(512)S(1)}, u32[]{:S(2)}) copy-start(f32[384]{0:T(512)S(1)} %get-tuple-element.346) | copy-start | bytes 4612
  9.2 70.2 %copy-start.92 = (f32[384]{0:T(512)}, f32[384]{0:T(512)S(1)}, u32[]{:S(2)}) copy-start(f32[384]{0:T(512)S(1)} %get-tuple-element.338) | copy-start | bytes 4612
  86.4 56.5 %copy-start.5 = (f32[2,576,384]{2,1,0:T(8,128)}, f32[2,576,384]{2,1,0:T(8,128)S(1)}, u32[]{:S(2)}) copy-start(f32[2,576,384]{2,1,0:T(8,128)S(1)} %get-tuple-element.523) | copy-start | bytes 5308420
  86.4 45.3 %copy-start.69 = (f32[1536]{0:T(1024)S(1)}, f32[1536]{0:T(1024)}, u32[]{:S(2)}) copy-start(f32[1536]{0:T(1024)} %param.37) | copy-start | bytes 18436
  99.2 43.7 %copy-start.44 = (f32[2,576]{1,0:T(2,128)}, f32[2,576]{1,0:T(2,128)S(1)}, u32[]{:S(2)}) copy-start(f32[2,576]{1,0:T(2,128)S(1)} %get-tuple-element.594) | copy-start | bytes 13828
  99.2 43.7 %copy-start.46 = (f32[2,576]{1,0:T(2,128)}, f32[2,576]{1,0:T(2,128)S(1)}, u32[]{:S(2)}) copy-start(f32[2,576]{1,0:T(2,128)S(1)} %get-tuple-element.595) | copy-start | bytes 13828
  100.5 140.2 %reduce-scatter.34.cloned.1.call-start = ((), (), s32[]{:S(2)}) async-start(), calls=%async_computation.22 | async-start | bytes 4423680
  142.9 18.7 %copy-start.7 = (f32[2,576,1536]{2,1,0:T(8,128)}, f32[2,576,1536]{2,1,0:T(8,128)S(1)}, u32[]{:S(2)}) copy-start(f32[2,576,1536]{2,1,0:T(8,128)S(1)} %get-tuple-element.638) | copy-start | bytes 21233668
  142.9 25.2 %copy-start.105 = (f32[1536]{0:T(1024)S(1)}, f32[1536]{0:T(1024)}, u32[]{:S(2)}) copy-start(f32[1536]{0:T(1024)} %param.38) | copy-start | bytes 18436
  142.9 26.5 %copy-start.120 = (f32[1536]{0:T(1024)S(1)}, f32[1536]{0:T(1024)}, u32[]{:S(2)}) copy-start(f32[1536]{0:T(1024)} %param.39) | copy-start | bytes 18436
  161.6 18.3 %copy-start.35 = (f32[2,1536]{1,0:T(2,128)}, f32[2,1536]{1,0:T(2,128)S(1)}, u32[]{:S(2)}) copy-start(f32[2,1536]{1,0:T(2,128)S(1)} %get-tuple-element.520) | copy-start | bytes 36868
  168.1 11.8 copy-start.131
  168.1 11.8 copy-start.113
  199.1 8.9 copy-start.28
  199.2 8.9 copy-start.117
  199.2 74.2 %all-gather.9.cloned.1.call-start = ((), (), s32[]{:S(2)}) async-start(), calls=%async_computation.13 | async-start | bytes 4423680 | tf_op jit(solution)/shard_map/all_gather | solution.py:41
  199.9 109.1 %all-gather.7.cloned.1.call-start = ((), (), s32[]{:S(2)}) async-start(), calls=%async_computation.12 | async-start | bytes 5038080 | tf_op jit(solution)/shard_map/all_gather | solution.py:41
  207.4 342.2 %copy-start.37 = (f32[2,384]{1,0:T(2,128)}, f32[2,384]{1,0:T(2,128)S(1)}, u32[]{:S(2)}) copy-start(f32[2,384]{1,0:T(2,128)S(1)} %fusion.70) | copy-start | bytes 9220
  208.1 51.4 %copy-start.50 = (f32[2,384]{1,0:T(2,128)}, f32[2,384]{1,0:T(2,128)S(1)}, u32[]{:S(2)}) copy-start(f32[2,384]{1,0:T(2,128)S(1)} %convolution_add_fusion) | copy-start | bytes 9220
  208.5 39.2 %copy-start.8 = (bf16[2,576,384]{2,1,0:T(8,128)(2,1)S(1)}, bf16[2,576,384]{2,1,0:T(8,128)(2,1)}, u32[]{:S(2)}) copy-start(bf16[2,576,384]{2,1,0:T(8,128)(2,1)} %param.28) | copy-start | bytes 2654212
  208.5 39.2 %copy-start.71 = (f32[384]{0:T(512)S(1)}, f32[384]{0:T(512)}, u32[]{:S(2)}) copy-start(f32[384]{0:T(512)} %param.41) | copy-start | bytes 4612
  247.7 12.3 copy-start.10
  261.1 217.1 %reduce-scatter.36.cloned.1.call-start = ((), (), s32[]{:S(2)}) async-start(), calls=%async_computation.23 | async-start | bytes 4423680
  322.5 9.8 copy-start.17
  332.3 13.6 copy-start.29
  352.8 10.6 copy-start.119
  387.0 136.7 %reduce-scatter.38.cloned.1.call-start = ((), (), s32[]{:S(2)}) async-start(), calls=%async_computation.24 | async-start | bytes 5406720
  387.1 14.6 copy-start.33
  433.3 13.4 copy-start.30
  478.2 105.7 %all-gather.11.cloned.1.call-start = ((), (), s32[]{:S(2)}) async-start(), calls=%async_computation.14 | async-start | bytes 4423680 | tf_op jit(solution)/shard_map/all_gather | solution.py:41
  530.1 14.8 %copy-start.118 = (f32[384]{0:T(512)S(1)}, f32[384]{0:T(512)}, u32[]{:S(2)}) copy-start(f32[384]{0:T(512)} %param.54) | copy-start | bytes 4612
  549.6 34.2 %copy-start.98 = (f32[2,1536]{1,0:T(2,128)S(1)}, f32[2,1536]{1,0:T(2,128)}, u32[]{:S(2)}) copy-start(f32[2,1536]{1,0:T(2,128)} %copy-done.97) | copy-start | bytes 36868
  549.6 34.2 %copy-start.106 = (f32[1536]{0:T(1024)S(1)}, f32[1536]{0:T(1024)}, u32[]{:S(2)}) copy-start(f32[1536]{0:T(1024)} %param.38) | copy-start | bytes 18436
  552.0 44.5 %copy-start.36 = (f32[2,1536]{1,0:T(2,128)S(1)}, f32[2,1536]{1,0:T(2,128)}, u32[]{:S(2)}) copy-start(f32[2,1536]{1,0:T(2,128)} %copy-done.35) | copy-start | bytes 36868
  552.0 50.5 %copy-start.132 = (f32[2]{0:T(128)S(1)}, f32[2]{0:T(128)}, u32[]{:S(2)}) copy-start(f32[2]{0:T(128)} %copy-done.131) | copy-start | bytes 28
  552.0 50.5 %copy-start.114 = (f32[2]{0:T(128)S(1)}, f32[2]{0:T(128)}, u32[]{:S(2)}) copy-start(f32[2]{0:T(128)} %copy-done.113) | copy-start | bytes 28
  552.0 50.6 %copy-start.40 = (f32[2,576]{1,0:T(2,128)S(1)}, f32[2,576]{1,0:T(2,128)}, u32[]{:S(2)}) copy-start(f32[2,576]{1,0:T(2,128)} %copy-done.39) | copy-start | bytes 13828
  552.0 50.6 %copy-start.52 = (f32[2,1536]{1,0:T(2,128)S(1)}, f32[2,1536]{1,0:T(2,128)}, u32[]{:S(2)}) copy-start(f32[2,1536]{1,0:T(2,128)} %get-tuple-element.518) | copy-start | bytes 36868
  552.0 50.6 %copy-start.70 = (f32[1536]{0:T(1024)S(1)}, f32[1536]{0:T(1024)}, u32[]{:S(2)}) copy-start(f32[1536]{0:T(1024)} %param.37) | copy-start | bytes 18436
  552.1 154.7 %reduce-scatter.40.cloned.1.call-start = ((), (), s32[]{:S(2)}) async-start(), calls=%async_computation.25 | async-start | bytes 4423680
  644.5 365.0 %reduce-scatter.26.cloned.1.call-start = ((), (), s32[]{:S(2)}) async-start(), calls=%async_computation.18 | async-start | bytes 2654208 | tf_op jit(solution)/shard_map/reduce_scatter | solution.py:315
  651.5 358.0 %reduce-scatter.28.cloned.1.call-start = ((), (), s32[]{:S(2)}) async-start(), calls=%async_computation.19 | async-start | bytes 2654208 | tf_op jit(solution)/shard_map/reduce_scatter | solution.py:316
  659.8 349.7 %reduce-scatter.30.cloned.1.call-start = ((), (), s32[]{:S(2)}) async-start(), calls=%async_computation.20 | async-start | bytes 2654208 | tf_op jit(solution)/shard_map/reduce_scatter | solution.py:317
  667.4 342.2 %reduce-scatter.32.cloned.1.call-start = ((), (), s32[]{:S(2)}) async-start(), calls=%async_computation.21 | async-start | bytes 2654208 | tf_op jit(solution)/shard_map/reduce_scatter | solution.py:319
  674.2 374.7 %all-reduce.25.cloned.1.call-start = ((), (), s32[]{:S(2)}) async-start(), calls=%async_computation.26 | async-start | bytes 393216 | tf_op jit(solution)/shard_map/psum | solution.py:321
  676.7 444.8 %reduce-scatter.24.cloned.1.call-start = ((), (), s32[]{:S(2)}) async-start(), calls=%async_computation.17 | async-start | bytes 2654208 | tf_op jit(solution)/shard_map/reduce_scatter | solution.py:318
  680.4 608.2 %reduce-scatter.20.cloned.1.call-start = ((), (), s32[]{:S(2)}) async-start(), calls=%async_computation.15 | async-start | bytes 10616832 | tf_op jit(solution)/shard_map/reduce_scatter | solution.py:313
  692.2 763.4 %reduce-scatter.22.cloned.1.call-start = ((), (), s32[]{:S(2)}) async-start(), calls=%async_computation.16 | async-start | bytes 10616832 | tf_op jit(solution)/shard_map/reduce_scatter | solution.py:314
  710.3 15.6 %copy-start.62 = (pred[2,576]{1,0:T(4,128)(4,1)S(1)}, pred[2,576]{1,0:T(4,128)(4,1)}, u32[]{:S(2)}) copy-start(pred[2,576]{1,0:T(4,128)(4,1)} %copy-done.61) | copy-start | bytes 3460
  868.5 23.0 %copy-start.2 = (f32[2,656,384]{2,1,0:T(8,128)S(1)}, f32[2,656,384]{2,1,0:T(8,128)}, u32[]{:S(2)}) copy-start(f32[2,656,384]{2,1,0:T(8,128)} %get-tuple-element.132) | copy-start | bytes 6045700
  918.9 23.1 %copy-start.3 = (f32[2,656,384]{2,1,0:T(8,128)S(1)}, f32[2,656,384]{2,1,0:T(8,128)}, u32[]{:S(2)}) copy-start(f32[2,656,384]{2,1,0:T(8,128)} %get-tuple-element.148) | copy-start | bytes 6045700
  984.1 22.7 %copy-start.16 = (f32[2,576,384]{2,1,0:T(8,128)S(1)}, f32[2,576,384]{2,1,0:T(8,128)}, u32[]{:S(2)}) copy-start(f32[2,576,384]{2,1,0:T(8,128)} %copy-done.15) | copy-start | bytes 5308420
  984.1 22.7 %copy-start.38 = (f32[2,384]{1,0:T(2,128)S(1)}, f32[2,384]{1,0:T(2,128)}, u32[]{:S(2)}) copy-start(f32[2,384]{1,0:T(2,128)} %copy-done.37) | copy-start | bytes 9220
  1006.7 451.9 %copy-start.1 = (bf16[1536,384]{1,0:T(8,128)(2,1)S(1)}, bf16[1536,384]{1,0:T(8,128)(2,1)}, u32[]{:S(2)}) copy-start(bf16[1536,384]{1,0:T(8,128)(2,1)} %param.50) | copy-start | bytes 3538948
  (85 other events, 357.1 us)
Sparse Core Ops, SparseCore 0:
  100.6 31.0 all-gather.4
  199.3 41.3 reduce-scatter.33
  242.4 30.9 all-gather.8
  275.5 33.4 all-gather.6
  387.1 40.4 reduce-scatter.35
  478.3 45.4 reduce-scatter.37
  552.1 31.7 all-gather.10
  644.7 41.4 reduce-scatter.39
  690.3 69.0 reduce-scatter.25
  763.3 67.9 reduce-scatter.27
  835.4 68.0 reduce-scatter.29
  907.4 68.4 reduce-scatter.31
  979.8 69.0 all-reduce.24
  1053.3 68.2 reduce-scatter.23
  1126.0 162.4 reduce-scatter.19
  1293.0 162.5 reduce-scatter.21
where the time goes:
time: 1480 us; the launch traced here: 1470 us
  waiting for transfers between devices  624 us (42%)
  local copies, waits for them, and re-layouts  303 us (20%)
  other arithmetic  225 us (15%)
  matrix products  193 us (13%)
  blocking collectives  103 us (7%)
  between operations  15.9 us (1%)
    reduce_scatter x1, waiting for transfers between devices, local(): lax.psum_scatter(mixer_contract_gradient, 'dp', scatter_dimension=1, tile...  167 us
    reduce_scatter x1, waiting for transfers between devices, local(): lax.psum_scatter(grad_ffn_in, 'dp', scatter_dimension=0, tiled=True)  167 us
    unnamed x307, local copies, waits for them, and re-layouts  139 us
    scatter-add x36, other arithmetic  110 us
    all_gather x4, waiting for transfers between devices, gather_rows(): return lax.all_gather(values, 'chan', axis=2, tiled=True)  105 us
    scatter-add x54, local copies, waits for them, and re-layouts  95.4 us
    unnamed x20, waiting for transfers between devices  73.1 us
    reduce_scatter x1, waiting for transfers between devices, local(): lax.psum_scatter(grad_text_weight, 'dp', scatter_dimension=0, tiled=True)  72.6 us
  transfers between devices with their start and end apart: 16, of which 10 were waited for; matrix products, arithmetic and copies ran while one was open for 28% of the time, Pallas kernels for 0%

commit v1 on v0

v1 whole, which is shorter than its diff:
```python
import functools

import jax
import jax.numpy as jnp
import numpy as np
from jax import lax
from jax.experimental import pallas as pl
from jax.experimental.pallas import tpu as pltpu
from jax.sharding import PartitionSpec as P

BF = jnp.bfloat16
F32 = jnp.float32
HEAD = 64
LANE = 128
EXTRA = 16
MARGIN = 40
WIDTHS = (36, 24, 18)
EPS = 1e-6

VM = pl.BlockSpec(memory_space=pltpu.VMEM)
SM = pl.BlockSpec(memory_space=pltpu.SMEM)
ANY = pl.BlockSpec(memory_space=pl.ANY)


def kernel_call(body, name, outs, args, in_specs, out_specs, grid=(1,), scratch=(), flops=0, limit=56):
    moved = sum(int(np.prod(a.shape)) * a.dtype.itemsize for a in tuple(args) + tuple(outs))
    return pl.pallas_call(
        body,
        name=name,
        out_shape=outs,
        grid=grid,
        in_specs=in_specs,
        out_specs=out_specs,
        scratch_shapes=scratch,
        compiler_params=pltpu.CompilerParams(vmem_limit_bytes=limit << 20),
        cost_estimate=pl.CostEstimate(
            flops=int(flops), bytes_accessed=int(moved), transcendentals=0
        ),
    )(*args)


def sds(shape, dtype):
    return jax.ShapeDtypeStruct(shape, dtype)


def nn(a, b):
    return jnp.dot(a, b, preferred_element_type=F32)


def nt(a, b):
    return lax.dot_general(a, b, (((1,), (1,)), ((), ())), preferred_element_type=F32)


def tn(a, b):
    return lax.dot_general(a, b, (((0,), (0,)), ((), ())), preferred_element_type=F32)


def eye():
    return (
        lax.broadcasted_iota(jnp.int32, (LANE, LANE), 0)
        == lax.broadcasted_iota(jnp.int32, (LANE, LANE), 1)
    ).astype(F32)


def col_to_tile(col):
    size = col.shape[0]
    diag = eye()
    row = lax.broadcasted_iota(jnp.int32, (8, LANE), 0)
    tile = jnp.zeros((8, LANE), F32)
    for t in range(pl.cdiv(size, LANE)):
        n = min(LANE, size - t * LANE)
        line = jnp.sum(col[t * LANE : t * LANE + n] * diag[:n], axis=0, keepdims=True)
        tile = jnp.where(row == t, line, tile)
    return tile


def tile_to_col(tile, size):
    diag = eye()
    cols = []
    for t in range(pl.cdiv(size, LANE)):
        n = min(LANE, size - t * LANE)
        cols.append(jnp.sum(tile[t : t + 1] * diag[:n], axis=1, keepdims=True))
    return jnp.concatenate(cols, axis=0)


def split_stats(both):
    high = both.astype(BF)
    rest = both - high.astype(F32)
    mid = rest.astype(BF)
    low = (rest - mid.astype(F32)).astype(BF)
    return jnp.concatenate([high, mid, low], axis=1)


def join_stats(tile):
    wide = tile.astype(F32)
    return wide[:, :LANE] + wide[:, LANE : 2 * LANE] + wide[:, 2 * LANE : 3 * LANE]


def stats_tile(first, second):
    return split_stats(jnp.concatenate([col_to_tile(first), col_to_tile(second)], axis=0))


def block_copies(me, refs, dst, sems, width, rows=None):
    copies = []
    for k, ref in enumerate(refs):
        place = pl.multiple_of((me ^ k) * width, LANE)
        target = dst.at[:, pl.ds(place, width)] if rows is None else dst.at[rows, pl.ds(place, width)]
        copies.append(pltpu.make_async_copy(ref, target, sems.at[k]))
    return copies


def scatter_copies(me, part, send, keep, sems, width):
    copies = []
    for k, dst in enumerate((keep.at[0], send.at[0], keep.at[1], send.at[1])):
        place = pl.multiple_of((me ^ k) * width, LANE)
        copies.append(pltpu.make_async_copy(part.at[:, pl.ds(place, width)], dst, sems.at[k]))
    return copies


def run_copies(copies):
    for c in copies:
        c.start()
    for c in copies:
        c.wait()


def norm_rows(raw, out, stat, size, width, blocks):
    total = width * blocks
    means = []
    for b in range(blocks):
        means.append(tile_to_col(raw[size : size + 8, b * width : b * width + LANE].astype(F32), size))
    mean_sum = jnp.zeros((size, 1), F32)
    for b in range(blocks):
        part = raw[:size, b * width : (b + 1) * width].astype(F32)
        mean_sum = mean_sum + jnp.sum(part, axis=1, keepdims=True) + width * means[b]
    mean = mean_sum * (1.0 / total)
    square = jnp.zeros((size, 1), F32)
    for b in range(blocks):
        part = raw[:size, b * width : (b + 1) * width].astype(F32) + (means[b] - mean)
        square = square + jnp.sum(part * part, axis=1, keepdims=True)
    inverse = lax.rsqrt(square * (1.0 / total) + EPS)
    for b in range(blocks):
        part = raw[:size, b * width : (b + 1) * width].astype(F32) + (means[b] - mean)
        out[:size, b * width : (b + 1) * width] = (part * inverse).astype(BF)
    stat[0] = jnp.broadcast_to(mean, (size, LANE))
    stat[1] = jnp.broadcast_to(inverse, (size, LANE))


def send_rows(values, pay, size, width):
    mean = jnp.mean(values, axis=1, keepdims=True).astype(BF).astype(F32)
    pay[:size] = (values - mean).astype(BF)
    tile = col_to_tile(mean).astype(BF)
    pay[size:] = jnp.zeros((EXTRA, width), BF)
    pay[size : size + EXTRA, :LANE] = jnp.concatenate([tile, jnp.zeros((8, LANE), BF)], axis=0)


def column_masks(size, width):
    slot = lax.broadcasted_iota(jnp.int32, (size, 1), 0).astype(F32)
    col = slot - width * jnp.floor((slot + 0.5) * (1.0 / width))
    return col > 0.5, col < width - 1.5


def conv_forward_body(l, info, x_ref, taps, bias, pay, conv, pad):
    size, width = conv.shape
    slot = lax.broadcasted_iota(jnp.int32, (size, 1), 0)
    x = jnp.where(slot < info[l, 0], x_ref[...].astype(F32), 0.0)
    pad[:MARGIN] = jnp.zeros((MARGIN, width), F32)
    pad[MARGIN + size :] = jnp.zeros((MARGIN, width), F32)
    here = slice(MARGIN, MARGIN + size)
    for bucket, w in enumerate(WIDTHS):

        @pl.when(info[l, 1] == bucket)
        def _():
            not_first, not_last = column_masks(size, w)
            pad[here] = x
            left = jnp.where(not_first, pad[MARGIN - 1 : MARGIN - 1 + size], 0.0)
            right = jnp.where(not_last, pad[MARGIN + 1 : MARGIN + 1 + size], 0.0)
            total = bias[...] + left * taps[3:4] + x * taps[4:5] + right * taps[5:6]
            pad[here] = left * taps[0:1] + x * taps[1:2] + right * taps[2:3]
            total = total + pad[MARGIN - w : MARGIN - w + size]
            pad[here] = left * taps[6:7] + x * taps[7:8] + right * taps[8:9]
            conv[...] = total + pad[MARGIN + w : MARGIN + w + size]

    send_rows(conv[...], pay, size, width)


def conv_backward_body(l, info, keep, got, far, conv, stat, x_ref, first_grad, taps, out, sums, pad, total_width):
    size, width = conv.shape
    slot = lax.broadcasted_iota(jnp.int32, (size, 1), 0)
    mask = slot < info[l, 0]
    grad = keep[:size].astype(F32) + got[:size].astype(F32) + far[:size].astype(F32)
    both = join_stats(keep[size:]) + join_stats(got[size:]) + join_stats(far[size:])
    both = both * (1.0 / total_width)
    mean_grad = tile_to_col(both[:8], size)
    mean_cross = tile_to_col(both[8:], size)
    mean = stat[0][:, :1]
    inverse = stat[1][:, :1]
    normed = (conv[...] - mean) * inverse
    grad = inverse * (grad - mean_grad - normed * mean_cross)
    x = jnp.where(mask, x_ref[...].astype(F32), 0.0)
    pad[:MARGIN] = jnp.zeros((MARGIN, width), F32)
    pad[MARGIN + size :] = jnp.zeros((MARGIN, width), F32)
    here = slice(MARGIN, MARGIN + size)
    sums[...] = jnp.zeros_like(sums)
    sums[9:10] = jnp.sum(grad, axis=0, keepdims=True)
    for bucket, w in enumerate(WIDTHS):

        @pl.when(info[l, 1] == bucket)
        def _():
            not_first, not_last = column_masks(size, w)
            pad[here] = x
            left = jnp.where(not_first, pad[MARGIN - 1 : MARGIN - 1 + size], 0.0)
            right = jnp.where(not_last, pad[MARGIN + 1 : MARGIN + 1 + size], 0.0)
            pad[here] = grad
            rows = (pad[MARGIN + w : MARGIN + w + size], grad, pad[MARGIN - w : MARGIN - w + size])
            for r in range(3):
                for c, side in enumerate((left, x, right)):
                    tap = 3 * r + c
                    sums[tap : tap + 1] = jnp.sum(rows[r] * side, axis=0, keepdims=True)
            back = [sum(rows[r] * taps[3 * r + c : 3 * r + c + 1] for r in range(3)) for c in range(3)]
            pad[here] = jnp.where(not_first, back[0], 0.0)
            total = back[1] + pad[MARGIN + 1 : MARGIN + 1 + size]
            pad[here] = jnp.where(not_last, back[2], 0.0)
            total = total + pad[MARGIN - 1 : MARGIN - 1 + size]
            out[...] = (first_grad[...] + jnp.where(mask, total, 0.0)).astype(BF)


def gelu_both(h):
    t_den = 1.0 + (0.3275911 * 0.7071067811865476) * jnp.abs(h)
    t = pl.reciprocal(t_den, approx=True)
    t = t * (2.0 - t_den * t)
    bell = jnp.exp(-0.5 * h * h)
    poly = t * (
        0.127414796 + t * (-0.142248368 + t * (0.7107068705 + t * (-0.7265760135 + t * 0.5307027145)))
    )
    tail = poly * bell
    phi = jnp.where(h >= 0, 1.0 - tail, tail)
    return h * phi, phi + h * bell * 0.3989422804014327


def ffn_in_body(l, lats, info, b0, b1, b2, b3, w, bias, nrm, stat, act, slope, spat, total, raw, sems, width, chunk):
    j = pl.program_id(0)
    size = nrm.shape[0]

    @pl.when(j == 0)
    def _():
        run_copies(block_copies(info[lats, 0], (b0, b1, b2, b3), raw, sems, width))
        norm_rows(raw, nrm, stat, size, width, 4)
        total[...] = jnp.zeros_like(total)

    valid_from = size - size // 32
    cols = act.shape[1]
    square = jnp.zeros((1, cols), F32)
    for r in range(0, size, chunk):
        h = nn(nrm[r : r + chunk], w[...]) + bias[...]
        a, d = gelu_both(h)
        act[r : r + chunk] = a.astype(BF)
        slope[r : r + chunk] = d.astype(BF)
        sq = a * a
        if r + chunk > valid_from:
            slot = r + lax.broadcasted_iota(jnp.int32, (chunk, 1), 0)
            sq = jnp.where(slot < info[l, 0], sq, 0.0)
        square = square + jnp.sum(sq, axis=0, keepdims=True)
    here = jnp.sqrt(square)
    spat[...] = here
    total[...] = total[...] + jnp.sum(here)


def denominator(t0, t1, t2, t3, hidden_total):
    whole = t0[...] + t1[...] + t2[...] + t3[...]
    return whole[:1, :1] * (1.0 / hidden_total) + EPS


def ffn_out_body(lats, hidden_total, info, act, spat, t0, t1, t2, t3, gamma, beta, w, gated, send, keep, part, sems, width, chunk):
    j = pl.program_id(0)
    size = act.shape[0]

    @pl.when(j == 0)
    def _():
        gain = 1.0 + gamma[...] * (spat[...] / denominator(t0, t1, t2, t3, hidden_total))
        for r in range(0, size, chunk):
            rows = slice(r, r + chunk)
            gated[rows] = (act[rows].astype(F32) * gain + beta[...]).astype(BF)

    cols = w.shape[1]
    part[:, pl.ds(pl.multiple_of(j * cols, LANE), cols)] = nn(gated[...], w[...]).astype(BF)

    @pl.when(j == pl.num_programs(0) - 1)
    def _():
        run_copies(scatter_copies(info[lats, 0], part, send, keep, sems, width))


def add_body(stats, keep, got, out):
    size = out.shape[0] - (EXTRA if stats else 0)
    out[:size] = (keep[:size].astype(F32) + got[:size].astype(F32)).astype(BF)
    if stats:
        out[size:] = split_stats(join_stats(keep[size:]) + join_stats(got[size:]))


def middle_body(x, keep, got, far, out_bias, scale, shift, first, pay):
    size, width = first.shape
    value = x[...].astype(F32) + (
        keep[...].astype(F32) + got[...].astype(F32) + far[...].astype(F32) + out_bias[...]
    )
    first[...] = value
    send_rows(value * (1.0 + scale[...]) + shift[...], pay, size, width)


def text_body(lats, info, b0, b1, b2, b3, w, bias, full, low, sems, width, text_len):
    lat_count, rows, _ = low.shape
    copies = []
    for l in range(lat_count):
        for k, ref in enumerate((b0, b1, b2, b3)):
            place = pl.multiple_of((info[lats, 0] ^ k) * width, LANE)
            copies.append(
                pltpu.make_async_copy(ref.at[l], full.at[l, :, pl.ds(place, width)], sems.at[4 * l + k])
            )
    run_copies(copies)
    row = lax.broadcasted_iota(jnp.int32, (rows, 1), 0)
    for l in range(lat_count):
        low[l] = jnp.where(row < text_len, nn(full[l], w[...]) + bias[...], 0.0).astype(BF)


def attention_body(
    l, lats, info, p0, p1, p2, p3, x0, x1, x2, x3, g0, g1, g2, g3, wq, wk, wv, wo, q_bias, v_bias,
    ctx, stat, g_full, att, dqkv, send, keep, sums,
    raw, w_all, w_out, q_s, k_s, v_s, do_s, kt_s, vt_s, att_t, dq_t, scores, part, sems, width,
):
    me = info[lats, 0]
    size = att.shape[0]
    rows = ctx.shape[0]
    total = ctx.shape[1]
    text = rows - size
    factor = HEAD ** (-0.5)
    copy_in = block_copies(me, (p0, p1, p2, p3), raw, sems, width)
    for k, ref in enumerate((x0, x1, x2, x3)):
        place = pl.multiple_of((me ^ k) * width, LANE)
        copy_in.append(
            pltpu.make_async_copy(ref.at[l], ctx.at[size:, pl.ds(place, width)], sems.at[4 + k])
        )
    copy_w = [
        pltpu.make_async_copy(ref, w_all.at[:, k * width : (k + 1) * width], sems.at[8 + k])
        for k, ref in enumerate((wq, wk, wv))
    ]
    copy_g = [pltpu.make_async_copy(wo, w_out, sems.at[11])]
    for k, ref in enumerate((g0, g1, g2, g3)):
        place = pl.multiple_of((me ^ k) * width, LANE)
        copy_g.append(
            pltpu.make_async_copy(ref.at[l], g_full.at[:, pl.ds(place, width)], sems.at[12 + k])
        )
    for c in copy_in + copy_w + copy_g:
        c.start()
    for c in copy_in:
        c.wait()
    norm_rows(raw, ctx, stat, size, width, 4)
    for c in copy_w:
        c.wait()
    q_s[...] = ((nn(ctx[:size], w_all[:, :width]) + q_bias[...]).astype(BF).astype(F32) * factor).astype(BF)
    keys = nn(ctx[...], w_all[:, width : 2 * width]).astype(BF)
    k_s[...] = keys
    kt_s[...] = keys.T
    values = (nn(ctx[...], w_all[:, 2 * width :]) + v_bias[...]).astype(BF)
    v_s[...] = values
    vt_s[...] = values.T
    for c in copy_g:
        c.wait()
    do_s[...] = nt(g_full[...], w_out[...]).astype(BF)
    tail = (size - size // 32) // 8 * 8
    key_row = tail + lax.broadcasted_iota(jnp.int32, (rows - tail, 1), 0)
    key_ok = (key_row < info[l, 0]) | ((key_row >= size) & (key_row < size + info[l, 2]))

    def pair(p, carry):
        lo = pl.multiple_of(p * LANE, LANE)
        q2 = q_s[:, pl.ds(lo, LANE)]
        k2 = k_s[:, pl.ds(lo, LANE)]
        v2 = v_s[:, pl.ds(lo, LANE)]
        do2 = do_s[:, pl.ds(lo, LANE)]
        dks, dvs = [], []
        for half in range(2):
            lanes = slice(half * HEAD, (half + 1) * HEAD)
            line = pl.ds(pl.multiple_of(p * LANE + half * HEAD, HEAD), HEAD)
            qh, kh, vh, doh = q2[:, lanes], k2[:, lanes], v2[:, lanes], do2[:, lanes]
            scores[...] = nt(kh, qh)
            scores[tail:] = jnp.where(key_ok, scores[tail:], -1e30)
            top = jnp.max(scores[...], axis=0, keepdims=True)
            expo = jnp.exp(scores[...] - top)
            probs = expo * (1.0 / jnp.sum(expo, axis=0, keepdims=True))
            low = probs.astype(BF)
            att_t[line] = nn(vt_s[line], low)
            scores[...] = probs
            grad_p = nt(vh, doh)
            dvs.append(nn(low, doh))
            dot = jnp.sum(scores[...] * grad_p, axis=0, keepdims=True)
            grad_s = (scores[...] * (grad_p - dot)).astype(BF)
            dks.append(nn(grad_s, qh))
            dq_t[line] = nn(kt_s[line], grad_s) * factor
        dqkv[:, pl.ds(pl.multiple_of(width + lo, LANE), LANE)] = jnp.concatenate(dks, axis=1).astype(BF)
        dqkv[:, pl.ds(pl.multiple_of(2 * width + lo, LANE), LANE)] = jnp.concatenate(dvs, axis=1).astype(BF)
        return carry

    lax.fori_loop(0, width // LANE, pair, 0)
    att[...] = att_t[...].astype(BF).T
    dq = dq_t[...].astype(BF).T
    dqkv[:size, :width] = dq
    dqkv[size:, :width] = jnp.zeros((text, width), BF)
    sums[...] = jnp.zeros_like(sums)
    sums[0:1] = jnp.sum(dq.astype(F32), axis=0, keepdims=True)
    sums[1:2] = jnp.sum(dqkv[:, 2 * width :].astype(F32), axis=0, keepdims=True)
    first = jnp.zeros((size, 1), F32)
    second = jnp.zeros((size, 1), F32)
    cols = 256
    for n in range(0, total, cols):
        block = nt(dqkv[...], w_all[n : n + cols]).astype(BF)
        part[:rows, n : n + cols] = block
        wide = block[:size].astype(F32)
        first = first + jnp.sum(wide, axis=1, keepdims=True)
        second = second + jnp.sum(wide * ctx[:size, n : n + cols].astype(F32), axis=1, keepdims=True)
    tile = stats_tile(first, second)
    for b in range(4):
        part[rows:, b * width : (b + 1) * width] = tile
    run_copies(scatter_copies(me, part, send, keep, sems, width))


def project_body(lats, info, att, w, send, keep, part, sems, width):
    cols = 512
    for n in range(0, part.shape[1], cols):
        part[:, n : n + cols] = nn(att[...], w[:, n : n + cols]).astype(BF)
    run_copies(scatter_copies(info[lats, 0], part, send, keep, sems, width))


def result_body(first, scale, shift, keep, got, far, bias, out):
    second = first[...] * (1.0 + scale[...]) + shift[...]
    branch = keep[...].astype(F32) + got[...].astype(F32) + far[...].astype(F32) + bias[...]
    out[...] = (second + branch).astype(BF)


def second_grad_body(keep, got, far, g_ref, first_ref, stat, scale, shift, pay, first_grad, text, sums, total_width, text_len):
    size, width = first_grad.shape
    rows = keep.shape[0] - EXTRA
    both = join_stats(keep[rows:]) + join_stats(got[rows:]) + join_stats(far[rows:])
    both = both * (1.0 / total_width)
    mean_grad = tile_to_col(both[:8], size)
    mean_cross = tile_to_col(both[8:], size)
    grad = keep[:size].astype(F32) + got[:size].astype(F32) + far[:size].astype(F32)
    first = first_ref[...]
    gain = 1.0 + scale[...]
    inverse = stat[1][:, :1]
    normed = (first * gain + shift[...] - stat[0][:, :1]) * inverse
    upstream = g_ref[...].astype(F32)
    second_grad = upstream + inverse * (grad - mean_grad - normed * mean_cross)
    scaled = second_grad * gain
    pay[...] = scaled.astype(BF)
    first_grad[...] = scaled
    row = lax.broadcasted_iota(jnp.int32, (rows - size, 1), 0)
    tail = keep[size:rows].astype(F32) + got[size:rows].astype(F32) + far[size:rows].astype(F32)
    low = jnp.where(row < text_len, tail, 0.0).astype(BF)
    text[...] = low
    sums[...] = jnp.zeros_like(sums)
    sums[0:1] = jnp.sum(second_grad * first, axis=0, keepdims=True)
    sums[1:2] = jnp.sum(second_grad, axis=0, keepdims=True)
    sums[2:3] = jnp.sum(scaled, axis=0, keepdims=True)
    sums[3:4] = jnp.sum(low.astype(F32), axis=0, keepdims=True)
    sums[4:5] = jnp.sum(upstream, axis=0, keepdims=True)


def gated_grad_body(lats, info, b0, b1, b2, b3, w, act, gamma, spat, full, out, s1, s2, total, sems, width, chunk):
    j = pl.program_id(0)
    size = full.shape[0]

    @pl.when(j == 0)
    def _():
        run_copies(block_copies(info[lats, 0], (b0, b1, b2, b3), full, sems, width))
        total[...] = jnp.zeros_like(total)

    cols = out.shape[1]
    cross = jnp.zeros((1, cols), F32)
    plain = jnp.zeros((1, cols), F32)
    for r in range(0, size, chunk):
        grad = nt(full[r : r + chunk], w[...])
        out[r : r + chunk] = grad.astype(BF)
        cross = cross + jnp.sum(grad * act[r : r + chunk].astype(F32), axis=0, keepdims=True)
        plain = plain + jnp.sum(grad, axis=0, keepdims=True)
    s1[...] = cross
    s2[...] = plain
    total[...] = total[...] + jnp.sum(cross * gamma[...] * spat[...])


def hidden_grad_body(
    l, lats, hidden_total, info, gg, act, slope, spat, s1, gamma, t0, t1, t2, t3, c0, c1, c2, c3, w, nrm,
    hidden, send, keep, bias_sum, gamma_sum, part, acc, sems, width, chunk,
):
    j = pl.program_id(0)
    size = hidden.shape[0]

    @pl.when(j == 0)
    def _():
        den = denominator(t0, t1, t2, t3, hidden_total)
        cross = (c0[...] + c1[...] + c2[...] + c3[...])[:1, :1]
        response = spat[...] / den
        gamma_sum[...] = response * s1[...]
        grad_spat = gamma[...] * s1[...] / den - cross / (den * den) * (1.0 / hidden_total)
        gain = gamma[...] * response + 1.0
        pull = grad_spat / spat[...]
        total = jnp.zeros_like(bias_sum[...])
        for r in range(0, size, chunk):
            rows = slice(r, r + chunk)
            slot = r + lax.broadcasted_iota(jnp.int32, (chunk, 1), 0)
            active = jnp.where(slot < info[l, 0], act[rows].astype(F32), 0.0)
            grad = gg[rows].astype(F32) * gain + pull * active
            low = (grad * slope[rows].astype(F32)).astype(BF)
            hidden[rows] = low
            total = total + jnp.sum(low.astype(F32), axis=0, keepdims=True)
        bias_sum[...] = total
        acc[...] = jnp.zeros_like(acc)

    cols = w.shape[0]
    block = nt(hidden[...], w[...]).astype(BF)
    part[:size, pl.ds(pl.multiple_of(j * cols, LANE), cols)] = block
    wide = block.astype(F32)
    acc[0] = acc[0] + jnp.sum(wide, axis=1, keepdims=True)
    acc[1] = acc[1] + jnp.sum(wide * nrm[...].astype(F32), axis=1, keepdims=True)

    @pl.when(j == pl.num_programs(0) - 1)
    def _():
        tile = stats_tile(acc[0][:, :1], acc[1][:, :1])
        for b in range(4):
            part[size:, b * width : (b + 1) * width] = tile
        run_copies(scatter_copies(info[lats, 0], part, send, keep, sems, width))


def place_blocks(places, result, send, keep):
    half = keep.shape[0]
    rows = keep.shape[1]
    for s in range(half):
        keep[s] = result[pl.ds(pl.multiple_of(places[s] * rows, 16), rows), :]
        send[s] = result[pl.ds(pl.multiple_of(places[half + s] * rows, 16), rows), :]


def weight_grad_body(pairs, split, plan, places, *refs):
    lefts_rights = refs[:pairs]
    outs = refs[pairs:-1]
    result = refs[-1]
    j = pl.program_id(0)
    for step, terms in enumerate(plan):

        @pl.when(j == step)
        def _():
            total = None
            for left, right in terms:
                term = tn(lefts_rights[left][...], lefts_rights[right][...])
                total = term if total is None else total + term
            result[...] = total.astype(BF)

    if split:
        place_blocks(places, result, *outs)
    else:
        outs[0][...] = result[...]


def weight_grads(name, places, lefts, tiles, cols, dp):
    operands = list(lefts)
    specs = [VM] * len(lefts)
    plan = []
    flops = 0
    for terms in tiles:
        entry = []
        for left, right, start in terms:
            entry.append((left, right, start))
        plan.append(entry)
    rights = []
    for terms in plan:
        for _, right, _ in terms:
            if not any(right is r for r in rights):
                rights.append(right)
    body_plan = []
    for step, terms in enumerate(plan):
        entry = []
        for left, right, _ in terms:
            entry.append((left, len(lefts) + [right is r for r in rights].index(True)))
            flops += 2 * right.shape[0] * lefts[left].shape[1] * cols
        body_plan.append(entry)
    for right in rights:
        table = []
        last = 0
        for terms in plan:
            for _, r, start in terms:
                if r is right:
                    last = start // cols
            table.append(last)
        first = next(start // cols for terms in plan for _, r, start in terms if r is right)
        for i in range(len(table)):
            if not any(r is right for terms in plan[: i + 1] for _, r, _ in terms):
                table[i] = first

        def index(j, table=tuple(table)):
            place = jnp.int32(table[0])
            for i in range(1, len(table)):
                if table[i] != table[i - 1]:
                    place = jnp.where(j >= i, jnp.int32(table[i]), place)
            return (0, place)

        operands.append(right)
        specs.append(pl.BlockSpec((right.shape[0], cols), index))
    width = lefts[0].shape[1]
    wide = cols * len(tiles)
    split = places is not None
    if split:
        half = dp // 2
        shape = sds((half, width // dp, wide), BF)
        outs = (shape, shape)
        out_specs = (pl.BlockSpec((half, width // dp, cols), lambda j: (0, 0, j)),) * 2
        args = (places, *operands)
        body = functools.partial(weight_grad_body, len(operands), True, body_plan)
        in_specs = [SM] + specs
    else:
        outs = (sds((width, wide), BF),)
        out_specs = (pl.BlockSpec((width, cols), lambda j: (0, j)),)
        args = tuple(operands)
        body = functools.partial(weight_grad_body, len(operands), False, body_plan, None)
        in_specs = specs
    return kernel_call(
        body, name, outs, args, in_specs, out_specs, grid=(len(tiles),),
        scratch=[pltpu.VMEM((width, cols), BF)], flops=flops,
    )


def pack_early_body(lat_count, noise, *refs):
    second = refs[:lat_count]
    attn = refs[lat_count : 2 * lat_count]
    gam = refs[2 * lat_count : 3 * lat_count]
    bet = refs[3 * lat_count : 4 * lat_count]
    out = refs[-1]
    width = out.shape[1]
    r = noise.shape[0]
    out[...] = jnp.zeros_like(out)
    out[:r] = sum(noise[:, l : l + 1] * second[l][0:1] for l in range(lat_count))
    out[r : 2 * r] = sum(noise[:, l : l + 1] * second[l][1:2] for l in range(lat_count))
    base = 2 * r
    for i in range(5):
        out[base + i : base + i + 1] = sum(second[l][i : i + 1] for l in range(lat_count))
    for i in range(2):
        out[base + 5 + i : base + 6 + i] = sum(attn[l][i : i + 1] for l in range(lat_count))
    for k, group in enumerate((gam, bet)):
        whole = sum(g[...] for g in group)
        for b in range(whole.shape[1] // width):
            at = base + 8 + 4 * k + b
            out[at : at + 1] = whole[:, b * width : (b + 1) * width]


def pack_late_body(lat_count, *refs):
    conv = refs[:lat_count]
    bias = refs[lat_count : 2 * lat_count]
    out = refs[-1]
    width = out.shape[1]
    out[...] = sum(c[...] for c in conv)
    whole = sum(b[...] for b in bias)
    for b in range(whole.shape[1] // width):
        out[10 + b : 11 + b] = whole[:, b * width : (b + 1) * width]


def local(
    latents, valid_mask, bucket_ids, text_count, text_tokens, noise_embed, conv_kernel, conv_bias,
    mixer_expand_weight, ffn_in_bias, grn_gamma, grn_beta, mixer_contract_weight, ffn_out_bias,
    scale_weight, scale_bias, shift_weight, shift_bias, text_weight, text_bias, query_weight, query_bias,
    key_weight, value_weight, value_bias, attn_out, attn_out_bias, upstream,
):
    lats, size, width = latents.shape
    groups = lax.axis_size("chan")
    dp = lax.axis_size("dp")
    total = width * groups
    hidden = mixer_expand_weight.shape[1]
    hidden_total = hidden * groups
    text_len = text_tokens.shape[1]
    text_rows = pl.cdiv(text_len, 16) * 16
    rows = size + text_rows
    highest = lax.Precision.HIGHEST
    me = lax.axis_index("chan")

    def xswap(v):
        return lax.ppermute(v, "chan", [(i, i ^ 2) for i in range(groups)])

    def cswap(v):
        return lax.ppermute(v, "chan", [(i, i ^ 1) for i in range(groups)])

    def gather(v):
        near = cswap(v)
        far = xswap(v)
        return v, near, far, cswap(far)

    def line(v):
        return v.reshape(1, -1)

    info = jnp.stack(
        [jnp.sum(valid_mask, axis=1), bucket_ids, text_count, jnp.zeros_like(bucket_ids)], axis=1
    )
    info = jnp.concatenate([info, jnp.full((1, 4), me, jnp.int32)], axis=0).astype(jnp.int32)

    def lat_spec(l, *shape):
        return pl.BlockSpec((None,) + shape, lambda *_: (l,) + (0,) * len(shape))

    def part_spec(k, shape):
        return pl.BlockSpec((None,) + tuple(shape[1:]), lambda *_: (k, 0, 0))

    text_act = jax.nn.silu(text_tokens.astype(F32)).astype(BF)
    text_act = jnp.pad(text_act, ((0, 0), (0, text_rows - text_len), (0, 0)))
    text_blocks = gather(text_act)

    def conv_forward(l):
        return kernel_call(
            functools.partial(conv_forward_body, l), "conv_forward_%d" % l,
            (sds((size + EXTRA, width), BF), sds((size, width), F32)),
            (info, latents, conv_kernel, line(conv_bias)),
            [SM, lat_spec(l, size, width), VM, VM], (VM, VM),
            scratch=[pltpu.VMEM((size + 2 * MARGIN, width), F32)], flops=size * width * 40,
        )

    tile_cols = 256

    def ffn_in(l, blocks):
        n = hidden // tile_cols
        col = pl.BlockSpec((1, tile_cols), lambda j: (0, j))
        wide = pl.BlockSpec((size, tile_cols), lambda j: (0, j))
        return kernel_call(
            functools.partial(ffn_in_body, l, lats, width=width, chunk=size // 3), "ffn_in_%d" % l,
            (sds((size, total), BF), sds((2, size, LANE), F32), sds((size, hidden), BF),
             sds((size, hidden), BF), sds((1, hidden), F32), sds((8, LANE), F32)),
            (info, *blocks, mixer_expand_weight, line(ffn_in_bias)),
            [SM] + [ANY] * 4 + [pl.BlockSpec((total, tile_cols), lambda j: (0, j)), col],
            (VM, VM, wide, wide, col, VM), grid=(n,),
            scratch=[pltpu.VMEM((size + EXTRA, total), BF), pltpu.SemaphoreType.DMA((4,))],
            flops=2 * size * total * hidden * 2,
        )

    def ffn_out(l, act, spat, tots):
        n = total // tile_cols
        shape = sds((2, size, width), BF)
        return kernel_call(
            functools.partial(ffn_out_body, lats, hidden_total, width=width, chunk=32), "ffn_out_%d" % l,
            (sds((size, hidden), BF), shape, shape),
            (info, act, spat, *tots, line(grn_gamma), line(grn_beta), mixer_contract_weight),
            [SM] + [VM] * 8 + [pl.BlockSpec((hidden, tile_cols), lambda j: (0, j))],
            (VM, ANY, ANY), grid=(n,),
            scratch=[pltpu.VMEM((size, total), BF), pltpu.SemaphoreType.DMA((4,))],
            flops=2 * size * total * hidden * 1.3,
        )

    def add_blocks(name, keep, got, stats):
        spec = part_spec(1, keep.shape)
        return kernel_call(
            functools.partial(add_body, stats), name, (sds(keep.shape[1:], BF),), (keep, got),
            [spec, spec], (VM,), grid=(1,), flops=keep.size,
        )[0]

    def scatter(name, send, keep, stats):
        got = cswap(send)
        far = xswap(add_blocks(name, keep, got, stats))
        return keep, got, far

    scale_rows = (jnp.dot(noise_embed, scale_weight, precision=highest) + scale_bias)[:, None]
    shift_rows = (jnp.dot(noise_embed, shift_weight, precision=highest) + shift_bias)[:, None]

    def middle(l, pieces):
        keep, got, far = pieces
        spec = part_spec(0, keep.shape)
        row = lat_spec(l, 1, width)
        return kernel_call(
            middle_body, "middle_%d" % l,
            (sds((size, width), F32), sds((size + EXTRA, width), BF)),
            (latents, keep, got, far, line(ffn_out_bias), scale_rows, shift_rows),
            [lat_spec(l, size, width), spec, spec, VM, VM, row, row], (VM, VM), grid=(1,),
            flops=size * width * 20,
        )

    def text_low_rows(blocks):
        return kernel_call(
            functools.partial(text_body, lats, width=width, text_len=text_len), "text_rows",
            (sds((lats, text_rows, total), BF), sds((lats, text_rows, width), BF)),
            (info, *blocks, text_weight, line(text_bias)),
            [SM] + [ANY] * 4 + [VM, VM], (VM, VM),
            scratch=[pltpu.SemaphoreType.DMA((4 * lats,))], flops=2 * lats * text_rows * total * width,
        )

    def attention(l, blocks, texts, grads):
        shape = sds((2, rows + EXTRA, width), BF)
        return kernel_call(
            functools.partial(attention_body, l, lats, width=width), "attention_%d" % l,
            (sds((rows, total), BF), sds((2, size, LANE), F32), sds((size, total), BF),
             sds((size, width), BF), sds((rows, 3 * width), BF), shape, shape, sds((8, width), F32)),
            (info, *blocks, *texts, *grads, query_weight, key_weight, value_weight, attn_out,
             line(query_bias), line(value_bias)),
            [SM] + [ANY] * 16 + [VM, VM],
            (VM, VM, VM, VM, VM, ANY, ANY, VM),
            scratch=[
                pltpu.VMEM((size + EXTRA, total), BF),
                pltpu.VMEM((total, 3 * width), BF),
                pltpu.VMEM((width, total), BF),
                pltpu.VMEM((size, width), BF),
                pltpu.VMEM((rows, width), BF),
                pltpu.VMEM((rows, width), BF),
                pltpu.VMEM((size, width), BF),
                pltpu.VMEM((width, rows), BF),
                pltpu.VMEM((width, rows), BF),
                pltpu.VMEM((width, size), F32),
                pltpu.VMEM((width, size), F32),
                pltpu.VMEM((rows, size), F32),
                pltpu.VMEM((rows + EXTRA, total), BF),
                pltpu.SemaphoreType.DMA((16,)),
            ],
            flops=2 * rows * total * width * 8 + 2 * rows * size * width * 24,
        )

    def project(l, att):
        shape = sds((2, size, width), BF)
        return kernel_call(
            functools.partial(project_body, lats, width=width), "project_%d" % l, (shape, shape),
            (info, att, attn_out), [SM, VM, VM], (ANY, ANY),
            scratch=[pltpu.VMEM((size, total), BF), pltpu.SemaphoreType.DMA((4,))],
            flops=2 * size * total * width,
        )

    def result_rows(l, first, pieces):
        keep, got, far = pieces
        spec = part_spec(0, keep.shape)
        row = lat_spec(l, 1, width)
        return kernel_call(
            result_body, "result_%d" % l, (sds((size, width), BF),),
            (first, scale_rows, shift_rows, keep, got, far, line(attn_out_bias)),
            [VM, row, row, spec, spec, VM, VM], (VM,), grid=(1,), flops=size * width * 6,
        )[0]

    def second_grad(l, pieces, first, stat):
        keep, got, far = pieces
        spec = part_spec(0, keep.shape)
        row = lat_spec(l, 1, width)
        return kernel_call(
            functools.partial(second_grad_body, total_width=total, text_len=text_len), "second_grad_%d" % l,
            (sds((size, width), BF), sds((size, width), F32), sds((text_rows, width), BF), sds((8, width), F32)),
            (keep, got, far, upstream, first, stat, scale_rows, shift_rows),
            [spec, spec, VM, lat_spec(l, size, width), VM, VM, row, row], (VM, VM, VM, VM), grid=(1,),
            flops=size * width * 30,
        )

    def gated_grad(l, blocks, act, spat):
        n = hidden // tile_cols
        col = pl.BlockSpec((1, tile_cols), lambda j: (0, j))
        wide = pl.BlockSpec((size, tile_cols), lambda j: (0, j))
        return kernel_call(
            functools.partial(gated_grad_body, lats, width=width, chunk=size // 3), "gated_grad_%d" % l,
            (sds((size, total), BF), sds((size, hidden), BF), sds((1, hidden), F32), sds((1, hidden), F32),
             sds((8, LANE), F32)),
            (info, *blocks, mixer_contract_weight, act, line(grn_gamma), spat),
            [SM] + [ANY] * 4 + [pl.BlockSpec((tile_cols, total), lambda j: (j, 0)), wide, col, col],
            (VM, wide, col, col, VM), grid=(n,),
            scratch=[pltpu.SemaphoreType.DMA((4,))], flops=2 * size * total * hidden * 1.3,
        )

    def hidden_grad(l, gg, act, slope, spat, s1, tots, crosses, nrm):
        n = total // tile_cols
        shape = sds((2, size + EXTRA, width), BF)
        return kernel_call(
            functools.partial(hidden_grad_body, l, lats, hidden_total, width=width, chunk=32),
            "hidden_grad_%d" % l,
            (sds((size, hidden), BF), shape, shape, sds((1, hidden), F32), sds((1, hidden), F32)),
            (info, gg, act, slope, spat, s1, line(grn_gamma), *tots, *crosses, mixer_expand_weight, nrm),
            [SM] + [VM] * 14
            + [pl.BlockSpec((tile_cols, hidden), lambda j: (j, 0)), pl.BlockSpec((size, tile_cols), lambda j: (0, j))],
            (VM, ANY, ANY, VM, VM), grid=(n,),
            scratch=[
                pltpu.VMEM((size + EXTRA, total), BF),
                pltpu.VMEM((2, size, LANE), F32),
                pltpu.SemaphoreType.DMA((4,)),
            ],
            flops=2 * size * total * hidden * 1.5,
        )

    def conv_backward(l, pieces, conv, stat, first_grad):
        keep, got, far = pieces
        spec = part_spec(0, keep.shape)
        return kernel_call(
            functools.partial(conv_backward_body, l, total_width=total), "conv_backward_%d" % l,
            (sds((size, width), BF), sds((16, width), F32)),
            (info, keep, got, far, conv, stat, latents, first_grad, conv_kernel),
            [SM, spec, spec, VM, VM, VM, lat_spec(l, size, width), VM, VM], (VM, VM), grid=(1,),
            scratch=[pltpu.VMEM((size + 2 * MARGIN, width), F32)], flops=size * width * 80,
        )

    half = dp // 2
    split = dp % 2 == 0 and 4 <= dp <= 16 and (total // dp) % 16 == 0
    if split:
        order = list(range(0, half, 2)) + list(range(half - 1 - half % 2, 0, -2))
        place_of = {z: p for p, z in enumerate(order)}
        table = np.zeros((dp, dp), np.int32)
        for d in range(dp):
            z, y = d // 2, d % 2
            for s in range(half):
                chunk = order[(place_of[z] - 1 - s) % half]
                table[d, s] = 2 * chunk + y
                table[d, half + s] = 2 * chunk + 1 - y
        places = lax.dynamic_index_in_dim(jnp.asarray(table), lax.axis_index("dp"), 0, keepdims=False)
        ring = [(2 * order[p] + y, 2 * order[(p + 1) % half] + y) for p in range(half) for y in range(2)]
    else:
        places = None

    def reduce_dp(parts):
        if not split:
            return lax.psum_scatter(parts[0], "dp", scatter_dimension=0, tiled=True).astype(F32)
        send, keep = parts
        got = lax.ppermute(send, "dp", [(i, i ^ 1) for i in range(dp)])
        moving = None
        for s in range(half):
            here = keep[s].astype(F32) + got[s].astype(F32)
            if moving is not None:
                here = here + moving.astype(F32)
            if s < half - 1:
                moving = lax.ppermute(here.astype(BF), "dp", ring)
        return here

    def sum_dp(v):
        if dp & (dp - 1):
            return lax.psum(v, "dp")
        step = 1
        while step < dp:
            v = v + lax.ppermute(v, "dp", [(i, i ^ step) for i in range(dp)])
            step *= 2
        return v

    every = range(lats)
    convs = [conv_forward(l) for l in every]
    pay1 = [gather(c[0]) for c in convs]
    text_full, text_low = text_low_rows(text_blocks)
    text_low_blocks = gather(text_low)
    up_blocks = gather(upstream)
    ffn = [ffn_in(l, pay1[l]) for l in every]
    tots = [gather(f[5]) for f in ffn]
    outs = [ffn_out(l, ffn[l][2], ffn[l][4], tots[l]) for l in every]
    gated = [o[0] for o in outs]
    mids = [middle(l, scatter("add_ffn_%d" % l, outs[l][1], outs[l][2], False)) for l in every]
    pay2 = [gather(m[1]) for m in mids]
    attn = [attention(l, pay2[l], text_low_blocks, up_blocks) for l in every]
    ctx_parts = [scatter("add_ctx_%d" % l, attn[l][5], attn[l][6], True) for l in every]
    seconds = [second_grad(l, ctx_parts[l], mids[l][0], attn[l][1]) for l in every]
    pay3 = [gather(s[0]) for s in seconds]
    projected = [project(l, attn[l][3]) for l in every]
    out_parts = [scatter("add_out_%d" % l, *projected[l], False) for l in every]
    result = jnp.stack([result_rows(l, mids[l][0], out_parts[l]) for l in every])

    cols = width
    tiles = []
    for k in range(3):
        tiles.append([(l, attn[l][4], k * width) for l in every])
    tiles.append([(lats + l, attn[l][3], 0) for l in every])
    lefts = [attn[l][0] for l in every] + [attn[l][2] for l in every]
    attn_grads = reduce_dp(weight_grads("attn_weight_grads", places, lefts, tiles, cols, dp))

    gg = [gated_grad(l, pay3[l], ffn[l][2], ffn[l][4]) for l in every]
    crosses = [gather(g[4]) for g in gg]
    lefts = [gg[l][0] for l in every] + [text_full[l] for l in every]
    tiles = [[(l, gated[l], k) for l in every] for k in range(0, hidden, cols)]
    tiles.append([(lats + l, seconds[l][2], 0) for l in every])
    mlp_grads = reduce_dp(weight_grads("contract_weight_grads", places, lefts, tiles, cols, dp))

    hid = [
        hidden_grad(l, gg[l][1], ffn[l][2], ffn[l][3], ffn[l][4], gg[l][2], tots[l], crosses[l], ffn[l][0])
        for l in every
    ]
    last_parts = [scatter("add_in_%d" % l, hid[l][1], hid[l][2], True) for l in every]
    lefts = [ffn[l][0] for l in every]
    tiles = [[(l, hid[l][0], k) for l in every] for k in range(0, hidden, cols)]
    in_grads = reduce_dp(weight_grads("expand_weight_grads", places, lefts, tiles, cols, dp))
    backs = [conv_backward(l, last_parts[l], convs[l][1], ffn[l][1], seconds[l][1]) for l in every]
    grad_latents = jnp.stack([b[0] for b in backs])

    noise_cols = noise_embed.T
    r = noise_embed.shape[1]
    early = kernel_call(
        functools.partial(pack_early_body, lats), "pack_early", (sds((2 * r + 16, width), F32),),
        (noise_cols, *[s[3] for s in seconds], *[a[7] for a in attn], *[h[4] for h in hid], *[g[3] for g in gg]),
        [VM] * (1 + 4 * lats), (VM,),
    )[0]
    early = sum_dp(early)
    late = kernel_call(
        functools.partial(pack_late_body, lats), "pack_late", (sds((16, width), F32),),
        (*[b[1] for b in backs], *[h[3] for h in hid]), [VM] * (2 * lats), (VM,),
    )[0]
    late = sum_dp(late)
    base = 2 * r
    return (
        result,
        grad_latents,
        late[:9],
        late[9],
        in_grads,
        late[10 : 10 + hidden // width].reshape(-1),
        early[base + 8 : base + 8 + hidden // width].reshape(-1),
        early[base + 12 : base + 12 + hidden // width].reshape(-1),
        mlp_grads[:, :hidden].T,
        early[base + 2],
        early[:r],
        early[base],
        early[r : 2 * r],
        early[base + 1],
        mlp_grads[:, hidden:],
        early[base + 3],
        attn_grads[:, :width],
        early[base + 5],
        attn_grads[:, width : 2 * width],
        attn_grads[:, 2 * width : 3 * width],
        early[base + 6],
        attn_grads[:, 3 * width :].T,
        early[base + 4],
    )


def solution(mesh):
    rows = P("dp", None, "chan")
    weight_in = P(None, "chan")
    vec = P("chan")
    in_specs = (
        rows, P("dp", None), P("dp"), P("dp"), rows, P("dp", None), weight_in, vec, weight_in, vec, vec, vec,
        P("chan", None), vec, weight_in, vec, weight_in, vec, weight_in, vec, weight_in, vec, weight_in,
        weight_in, vec, P("chan", None), vec, rows,
    )
    out_specs = (
        rows, rows, weight_in, vec, P("dp", "chan"), vec, vec, vec, P("chan", "dp"), vec, weight_in, vec,
        weight_in, vec, P("dp", "chan"), vec, P("dp", "chan"), vec, P("dp", "chan"), P("dp", "chan"), vec,
        P("chan", "dp"), vec,
    )
    return jax.shard_map(local, mesh=mesh, in_specs=in_specs, out_specs=out_specs, check_vma=False)
```

time: 1480 us -> 636 us (0.43)
  waiting for transfers between devices: 624 us -> 238 us
  Pallas kernels: 0 us -> 273 us
  local copies, waits for them, and re-layouts: 303 us -> 40.4 us
  other arithmetic: 225 us -> 22.6 us
  matrix products: 193 us -> 0.34 us
  blocking collectives: 103 us -> 0 us
  starting transfers between devices: 1.24 us -> 49.9 us
    reduce_scatter x7 -> x0, waiting for transfers between devices: 407 us -> none  [the longest x1 167 us: local(): lax.psum_scatter(mixer_contract_gradient, 'dp', scatter_dimension=1, tile...]
    pallas_call x0 -> x36, Pallas kernels: none -> 273 us  [kernel_call(): pl.pallas_call(body, name=name, out_shape=outs, grid=grid, in_specs=in_sp...]
    ppermute x0 -> x73, waiting for transfers between devices: none -> 238 us  [the longest x6 104 us: sum_dp(): v = v + lax.ppermute(v, 'dp', [(i, i ^ step) for i in range(dp)])]
    dot_general x28 -> x0, matrix products: 192 us -> none  [the longest x1 14.6 us: local(): jnp.einsum('lqhd,lkhd->lhqk', grad_attended, head_v, preferred_element_ty...]
    unnamed x307 -> x179, local copies, waits for them, and re-layouts: 139 us -> 22.4 us
    scatter-add x38 -> x0, other arithmetic: 111 us -> none
    all_gather x4 -> x0, waiting for transfers between devices: 105 us -> none  [gather_rows(): return lax.all_gather(values, 'chan', axis=2, tiled=True)]
    psum x7 -> x0, blocking collectives: 96.2 us -> none  [the longest x6 57.3 us: channel_stats(): return lax.psum(parts, 'chan')]
  transfers between devices with their start and end apart: 16 -> 73, of which waited for: 10 -> 20; matrix products, arithmetic and copies ran while one was open for 28% -> 5% of each run, Pallas kernels for 0% -> 43%
where the time goes in v1:
time: 636 us; the launch traced here: 626 us
  Pallas kernels  273 us (43%)
  waiting for transfers between devices  238 us (37%)
  starting transfers between devices  49.9 us (8%)
  local copies, waits for them, and re-layouts  40.4 us (6%)
  other arithmetic  22.6 us (4%)
    pallas_call x36, Pallas kernels, kernel_call(): pl.pallas_call(body, name=name, out_shape=outs, grid=grid, in_specs=in_sp...  273 us
    ppermute x6, waiting for transfers between devices, sum_dp(): v = v + lax.ppermute(v, 'dp', [(i, i ^ step) for i in range(dp)])  104 us
    ppermute x21, waiting for transfers between devices, xswap(): return lax.ppermute(v, 'chan', [(i, i ^ 2) for i in range(groups)])  82.8 us
    ppermute x9, waiting for transfers between devices, reduce_dp(): moving = lax.ppermute(here.astype(BF), 'dp', ring)  48.1 us
    unnamed x179, local copies, waits for them, and re-layouts  22.4 us
    ppermute x21, starting transfers between devices, xswap(): return lax.ppermute(v, 'chan', [(i, i ^ 2) for i in range(groups)])  20.5 us
    convert_element_type x9, other arithmetic, reduce_dp(): moving = lax.ppermute(here.astype(BF), 'dp', ring)  13.3 us
  transfers between devices with their start and end apart: 73, of which 20 were waited for; matrix products, arithmetic and copies ran while one was open for 5% of the time, Pallas kernels for 43%

profile of v1, /device:TPU:0, one launch (start us, length us, event | category | flops | bytes accessed | tf_op | source)
XLA Modules:
  0.0 626.5 jit_solution(506585578210950588)
XLA Ops:
  5.1 3.8 conv_forward_1.1
  8.9 2.9 collective-permute-start.23
  11.9 4.1 conv_forward_0.1
  16.0 7.4 %collective-permute-done.23.b2 = bf16[592,384]{1,0:T(8,128)(2,1)S(1)} collective-permute-done((bf16[592,384]{1,0:T(8,128)(2,1)}, bf16[592,384]{1,0:T(8,128)(2,1)S(1)}, u32[]{:S(2)}, u32[]{:S(2)}) %collective-permute-start.23) | collective-permute-done | bytes 454688 | tf_op jit(solution)/shard_map/ppermute | solution.py:680
  24.5 7.8 %collective-permute-done.1.b2 = bf16[592,384]{1,0:T(8,128)(2,1)S(1)} collective-permute-done((bf16[592,384]{1,0:T(8,128)(2,1)}, bf16[592,384]{1,0:T(8,128)(2,1)S(1)}, u32[]{:S(2)}, u32[]{:S(2)}) %collective-permute-start.1) | collective-permute-done | bytes 454688 | tf_op jit(solution)/shard_map/ppermute | solution.py:680
  33.9 13.9 %ffn_in_1.1 = (bf16[576,1536]{1,0:T(8,128)(2,1)}, f32[2,576,128]{2,1,0:T(8,128)}, bf16[576,1536]{1,0:T(8,128)(2,1)}, bf16[576,1536]{1,0:T(8,128)(2,1)}, f32[1,1536]{1,0:T(1,128)}, /*index=5*/f32[8,128]{1,0:T(8,128)}) custom-call(s32[3,4]{1,0:T(4,128)} %concatenate.3.info, bf16[592,384]{1,0:T(8,128)(2,1)} %get-tuple-element.121.b0, ...), custom_call_target="tpu_custom_call" | custom-call | flops 5435817984 | bytes 12451888 | tf_op jit(solution)/shard_map/ffn_in_1/pallas_call | solution.py:27
  47.8 1.8 collective-permute-start.26
  51.2 14.0 %ffn_in_0.1 = (bf16[576,1536]{1,0:T(8,128)(2,1)}, f32[2,576,128]{2,1,0:T(8,128)}, bf16[576,1536]{1,0:T(8,128)(2,1)}, bf16[576,1536]{1,0:T(8,128)(2,1)}, f32[1,1536]{1,0:T(1,128)}, /*index=5*/f32[8,128]{1,0:T(8,128)}) custom-call(s32[3,4]{1,0:T(4,128)} %concatenate.3.info, bf16[592,384]{1,0:T(8,128)(2,1)} %get-tuple-element.109.b0, ...), custom_call_target="tpu_custom_call" | custom-call | flops 5435817984 | bytes 12451888 | tf_op jit(solution)/shard_map/ffn_in_0/pallas_call | solution.py:27
  69.7 9.8 %ffn_out_1.1 = (bf16[576,1536]{1,0:T(8,128)(2,1)}, bf16[2,576,384]{2,1,0:T(8,128)(2,1)}, bf16[2,576,384]{2,1,0:T(8,128)(2,1)}) custom-call(s32[3,4]{1,0:T(4,128)} %concatenate.3.info, bf16[576,1536]{1,0:T(8,128)(2,1)} %get-tuple-element.122.act, f32[1,1536]{1,0:T(1,128)} %get-tuple-element.123.spat, f32[8,128]{1,0:T(8,128)} %get-tuple-element.124.t0, ...), custom_call_target="tpu_custom_call" | custom-call | flops 3533281792 | bytes 10061872 | tf_op jit(solution)/shard_map/ffn_out_1/pallas_call | solution.py:27
  80.7 10.3 %ffn_out_0.1 = (bf16[576,1536]{1,0:T(8,128)(2,1)}, bf16[2,576,384]{2,1,0:T(8,128)(2,1)}, bf16[2,576,384]{2,1,0:T(8,128)(2,1)}) custom-call(s32[3,4]{1,0:T(4,128)} %concatenate.3.info, bf16[576,1536]{1,0:T(8,128)(2,1)} %get-tuple-element.110.act, f32[1,1536]{1,0:T(1,128)} %get-tuple-element.111.spat, f32[8,128]{1,0:T(8,128)} %get-tuple-element.112.t0, ...), custom_call_target="tpu_custom_call" | custom-call | flops 3533281792 | bytes 10061872 | tf_op jit(solution)/shard_map/ffn_out_0/pallas_call | solution.py:27
  94.3 2.0 add_ffn_1.1
  97.8 2.0 add_ffn_0.1
  103.5 22.3 %collective-permute-done.29.far = bf16[576,384]{1,0:T(8,128)(2,1)S(1)} collective-permute-done((bf16[576,384]{1,0:T(8,128)(2,1)}, bf16[576,384]{1,0:T(8,128)(2,1)S(1)}, u32[]{:S(2)}, u32[]{:S(2)}) %collective-permute-start.29) | collective-permute-done | bytes 442400 | tf_op jit(solution)/shard_map/ppermute | solution.py:680
  126.5 2.8 middle_1.1
  130.9 2.7 collective-permute-done.13.b3
  134.3 3.5 text_rows.1
  139.6 7.5 %collective-permute-done.15.x2 = bf16[2,80,384]{2,1,0:T(8,128)(2,1)S(1)} collective-permute-done((bf16[2,80,384]{2,1,0:T(8,128)(2,1)}, bf16[2,80,384]{2,1,0:T(8,128)(2,1)S(1)}, u32[]{:S(2)}, u32[]{:S(2)}) %collective-permute-start.15) | collective-permute-done | bytes 122912 | tf_op jit(solution)/shard_map/ppermute | solution.py:680
  147.9 2.8 middle_0.1
  153.1 10.8 %collective-permute-done.9.p2 = bf16[592,384]{1,0:T(8,128)(2,1)S(1)} collective-permute-done((bf16[592,384]{1,0:T(8,128)(2,1)}, bf16[592,384]{1,0:T(8,128)(2,1)S(1)}, u32[]{:S(2)}, u32[]{:S(2)}) %collective-permute-start.9) | collective-permute-done | bytes 454688 | tf_op jit(solution)/shard_map/ppermute | solution.py:680
  165.8 28.6 %attention_1.1 = (bf16[656,1536]{1,0:T(8,128)(2,1)}, f32[2,576,128]{2,1,0:T(8,128)}, bf16[576,1536]{1,0:T(8,128)(2,1)}, bf16[576,384]{1,0:T(8,128)(2,1)}, bf16[6...) custom-call(s32[3,4]{1,0:T(4,128)} %concatenate.3.info, ...), custom_call_target="tpu_custom_call" | custom-call | flops 13155434496 | bytes 18975792 | tf_op jit(solution)/shard_map/attention_1/pallas_call | solution.py:27
  196.6 28.8 %attention_0.1 = (bf16[656,1536]{1,0:T(8,128)(2,1)}, f32[2,576,128]{2,1,0:T(8,128)}, bf16[576,1536]{1,0:T(8,128)(2,1)}, bf16[576,384]{1,0:T(8,128)(2,1)}, bf16[6...) custom-call(s32[3,4]{1,0:T(4,128)} %concatenate.3.info, ...), custom_call_target="tpu_custom_call" | custom-call | flops 13155434496 | bytes 18975792 | tf_op jit(solution)/shard_map/attention_0/pallas_call | solution.py:27
  226.4 2.1 add_ctx_1.1
  229.9 2.1 add_ctx_0.1
  232.0 1.7 collective-permute-start.36
  233.7 3.7 project_1.1
  239.5 3.8 project_0.1
  244.6 4.0 second_grad_1.1
  248.9 5.5 collective-permute-done.36.far
  255.2 4.1 second_grad_0.1
  260.9 3.0 collective-permute-done.48.b2
  263.9 9.1 %collective-permute-done.38.b2 = bf16[576,384]{1,0:T(8,128)(2,1)S(1)} collective-permute-done((bf16[576,384]{1,0:T(8,128)(2,1)}, bf16[576,384]{1,0:T(8,128)(2,1)S(1)}, u32[]{:S(2)}, u32[]{:S(2)}) %collective-permute-start.38) | collective-permute-done | bytes 442400 | tf_op jit(solution)/shard_map/ppermute | solution.py:680
  272.9 16.3 %attn_weight_grads.1 = (bf16[4,192,1536]{2,1,0:T(8,128)(2,1)}, bf16[4,192,1536]{2,1,0:T(8,128)(2,1)}) custom-call(s32[8]{0:T(128)} %dynamic-slice_bitcast_fusion.places, bf16[656,1536]{1,0:T(8,128)(2,1)} %get-tuple-element.187.refs_0_, bf16[656,1536]{1,0:T(8,128)(2,1)} %get-tuple-element.188.refs_1_, bf16[576,1536]{1,0:T(8,128)(2,1)} %get-tuple-element.189.refs_2_, ...), custom_call_target="tpu_custom_call" | custom-call | flops 6002049024 | bytes 16195616 | tf_op jit(solution)/shard_map/attn_weight_grads/pallas_call | solution.py:27
  289.2 2.0 add_out_1.1
  292.9 2.0 add_out_0.1
  296.4 10.8 %gated_grad_1.1 = (bf16[576,1536]{1,0:T(8,128)(2,1)}, bf16[576,1536]{1,0:T(8,128)(2,1)}, f32[1,1536]{1,0:T(1,128)}, f32[1,1536]{1,0:T(1,128)}, f32[8,128]{1,0:T(8,128)}) custom-call(s32[3,4]{1,0:T(4,128)} %concatenate.3.info, bf16[576,384]{1,0:T(8,128)(2,1)} %get-tuple-element.150.b0, bf16[576,384]{1,0:T(8,128)(2,1)} %copy-done.70, ...), custom_call_target="tpu_custom_call" | custom-call | flops 3533281792 | bytes 11825200 | tf_op jit(solution)/shard_map/gated_grad_1/pallas_call | solution.py:27
  310.1 10.8 %gated_grad_0.1 = (bf16[576,1536]{1,0:T(8,128)(2,1)}, bf16[576,1536]{1,0:T(8,128)(2,1)}, f32[1,1536]{1,0:T(1,128)}, f32[1,1536]{1,0:T(1,128)}, f32[8,128]{1,0:T(8,128)}) custom-call(s32[3,4]{1,0:T(4,128)} %concatenate.3.info, bf16[576,384]{1,0:T(8,128)(2,1)} %get-tuple-element.135.b0, bf16[576,384]{1,0:T(8,128)(2,1)} %copy-done.68, ...), custom_call_target="tpu_custom_call" | custom-call | flops 3533281792 | bytes 11825200 | tf_op jit(solution)/shard_map/gated_grad_0/pallas_call | solution.py:27
  321.7 15.4 %contract_weight_grads.1 = (bf16[4,192,1920]{2,1,0:T(8,128)(2,1)}, bf16[4,192,1920]{2,1,0:T(8,128)(2,1)}) custom-call(s32[8]{0:T(128)} %dynamic-slice_bitcast_fusion.places, bf16[576,1536]{1,0:T(8,128)(2,1)} %get-tuple-element.178.refs_0_, bf16[576,1536]{1,0:T(8,128)(2,1)} %get-tuple-element.179.refs_1_, bf16[80,1536]{1,0:T(8,128)(2,1)} %get-tuple-element.207.refs_2_, ...), custom_call_target="tpu_custom_call" | custom-call | flops 5624561664 | bytes 13590560 | tf_op jit(solution)/shard_map/contract_weight_grads/pallas_call | solution.py:27
  339.4 13.2 %hidden_grad_1.1 = (bf16[576,1536]{1,0:T(8,128)(2,1)}, bf16[2,592,384]{2,1,0:T(8,128)(2,1)}, bf16[2,592,384]{2,1,0:T(8,128)(2,1)}, f32[1,1536]{1,0:T(1,128)}, f32[1,1536]{1,0:T(1,128)}) custom-call(s32[3,4]{1,0:T(4,128)} %concatenate.3.info, bf16[576,1536]{1,0:T(8,128)(2,1)} %get-tuple-element.151.gg, bf16[576,1536]{1,0:T(8,128)(2,1)} %get-tuple-element.122.act, ...), custom_call_target="tpu_custom_call" | custom-call | flops 4076863488 | bytes 15448112 | tf_op jit(solution)/shard_map/hidden_grad_1/pallas_call | solution.py:27
  354.2 13.3 %hidden_grad_0.1 = (bf16[576,1536]{1,0:T(8,128)(2,1)}, bf16[2,592,384]{2,1,0:T(8,128)(2,1)}, bf16[2,592,384]{2,1,0:T(8,128)(2,1)}, f32[1,1536]{1,0:T(1,128)}, f32[1,1536]{1,0:T(1,128)}) custom-call(s32[3,4]{1,0:T(4,128)} %concatenate.3.info, bf16[576,1536]{1,0:T(8,128)(2,1)} %get-tuple-element.136.gg, bf16[576,1536]{1,0:T(8,128)(2,1)} %get-tuple-element.110.act, ...), custom_call_target="tpu_custom_call" | custom-call | flops 4076863488 | bytes 15448112 | tf_op jit(solution)/shard_map/hidden_grad_0/pallas_call | solution.py:27
  370.3 14.6 %expand_weight_grads.1 = (bf16[4,192,1536]{2,1,0:T(8,128)(2,1)}, bf16[4,192,1536]{2,1,0:T(8,128)(2,1)}) custom-call(s32[8]{0:T(128)} %dynamic-slice_bitcast_fusion.places, bf16[576,1536]{1,0:T(8,128)(2,1)} %get-tuple-element.140.nrm.refs_0_, bf16[576,1536]{1,0:T(8,128)(2,1)} %get-tuple-element.155.nrm.refs_1_, bf16[576,1536]{1,0:T(8,128)(2,1)} %get-tuple-element.166.refs_2_, ...), custom_call_target="tpu_custom_call" | custom-call | flops 5435817984 | bytes 11796512 | tf_op jit(solution)/shard_map/expand_weight_grads/pallas_call | solution.py:27
  385.9 38.5 %collective-permute-done.62 = f32[144,384]{1,0:T(8,128)S(1)} collective-permute-done((f32[144,384]{1,0:T(8,128)}, f32[144,384]{1,0:T(8,128)S(1)}, u32[]{:S(2)}, u32[]{:S(2)}) %collective-permute-start.62) | collective-permute-done | bytes 221216 | tf_op jit(solution)/shard_map/ppermute | solution.py:923
  424.4 2.6 collective-permute-start.70
  427.2 16.2 %collective-permute-done.63 = f32[144,384]{1,0:T(8,128)S(1)} collective-permute-done((f32[144,384]{1,0:T(8,128)S(1)}, f32[144,384]{1,0:T(8,128)S(1)}, u32[]{:S(2)}, u32[]{:S(2)}) %collective-permute-start.63) | collective-permute-done | bytes 221216 | tf_op jit(solution)/shard_map/ppermute | solution.py:923
  444.0 2.6 result_1.1
  446.6 2.6 result_0.1
  449.2 2.4 collective-permute-start.64
  451.9 10.8 %collective-permute-done.64 = f32[144,384]{1,0:T(8,128)S(1)} collective-permute-done((f32[144,384]{1,0:T(8,128)S(1)}, f32[144,384]{1,0:T(8,128)S(1)}, u32[]{:S(2)}, u32[]{:S(2)}) %collective-permute-start.64) | collective-permute-done | bytes 221216 | tf_op jit(solution)/shard_map/ppermute | solution.py:923
  464.9 2.0 add_in_1.1
  468.6 2.0 add_in_0.1
  472.7 7.8 %collective-permute-done.54.far = bf16[592,384]{1,0:T(8,128)(2,1)S(1)} collective-permute-done((bf16[592,384]{1,0:T(8,128)(2,1)}, bf16[592,384]{1,0:T(8,128)(2,1)S(1)}, u32[]{:S(2)}, u32[]{:S(2)}) %collective-permute-start.54) | collective-permute-done | bytes 454688 | tf_op jit(solution)/shard_map/ppermute | solution.py:680
  481.3 8.3 %conv_backward_1.1 = (bf16[576,384]{1,0:T(8,128)(2,1)}, f32[16,384]{1,0:T(8,128)}) custom-call(s32[3,4]{1,0:T(4,128)} %concatenate.3.info, bf16[2,592,384]{2,1,0:T(8,128)(2,1)} %get-tuple-element.156.keep, bf16[2,592,384]{2,1,0:T(8,128)(2,1)} %copy-done.5, bf16[592,384]{1,0:T(8,128)(2,1)} %copy-done.23, f32[576,384]{1,0:T(8,128)} %get-tuple-element.158.conv, ...), custom_call_target="tpu_custom_call" | custom-call | flops 17694720 | bytes 5998128 | tf_op jit(solution)/shard_map/conv_backward_1/pallas_call | solution.py:27
  490.4 7.9 %conv_backward_0.1 = (bf16[576,384]{1,0:T(8,128)(2,1)}, f32[16,384]{1,0:T(8,128)}) custom-call(s32[3,4]{1,0:T(4,128)} %concatenate.3.info, bf16[2,592,384]{2,1,0:T(8,128)(2,1)} %get-tuple-element.141.keep, bf16[2,592,384]{2,1,0:T(8,128)(2,1)} %copy-done.4, bf16[592,384]{1,0:T(8,128)(2,1)} %copy-done.22, f32[576,384]{1,0:T(8,128)} %get-tuple-element.143.conv, ...), custom_call_target="tpu_custom_call" | custom-call | flops 17694720 | bytes 5998128 | tf_op jit(solution)/shard_map/conv_backward_0/pallas_call | solution.py:27
  504.5 5.6 collective-permute-start.56
  510.1 2.6 fusion.3
  513.3 2.2 fusion.7
  515.5 2.9 collective-permute-start.59
  518.4 2.2 fusion.6
  523.1 37.2 %collective-permute-done.57 = f32[16,384]{1,0:T(8,128)S(1)} collective-permute-done((f32[16,384]{1,0:T(8,128)S(1)}, f32[16,384]{1,0:T(8,128)S(1)}, u32[]{:S(2)}, u32[]{:S(2)}) %collective-permute-start.57) | collective-permute-done | bytes 24608 | tf_op jit(solution)/shard_map/ppermute | solution.py:923
  565.0 1.8 bitcast_add_fusion.5
  566.7 12.7 %collective-permute-done.60 = bf16[192,1536]{1,0:T(8,128)(2,1)S(1)} collective-permute-done((bf16[192,1536]{1,0:T(8,128)(2,1)S(1)}, bf16[192,1536]{1,0:T(8,128)(2,1)S(1)}, u32[]{:S(2)}, u32[]{:S(2)}) %collective-permute-start.60) | collective-permute-done | bytes 589856 | tf_op jit(solution)/shard_map/ppermute | solution.py:915
  581.6 13.6 %collective-permute-done.67 = bf16[192,1920]{1,0:T(8,128)(2,1)S(1)} collective-permute-done((bf16[192,1920]{1,0:T(8,128)(2,1)S(1)}, bf16[192,1920]{1,0:T(8,128)(2,1)S(1)}, u32[]{:S(2)}, u32[]{:S(2)}) %collective-permute-start.67) | collective-permute-done | bytes 737312 | tf_op jit(solution)/shard_map/ppermute | solution.py:915
  598.6 9.3 %collective-permute-done.61 = bf16[192,1536]{1,0:T(8,128)(2,1)S(1)} collective-permute-done((bf16[192,1536]{1,0:T(8,128)(2,1)S(1)}, bf16[192,1536]{1,0:T(8,128)(2,1)S(1)}, u32[]{:S(2)}, u32[]{:S(2)}) %collective-permute-start.61) | collective-permute-done | bytes 589856 | tf_op jit(solution)/shard_map/ppermute | solution.py:915
  607.8 2.3 bitcast_add_fusion.8
  610.1 12.6 %collective-permute-done.68 = bf16[192,1920]{1,0:T(8,128)(2,1)S(1)} collective-permute-done((bf16[192,1920]{1,0:T(8,128)(2,1)S(1)}, bf16[192,1920]{1,0:T(8,128)(2,1)S(1)}, u32[]{:S(2)}, u32[]{:S(2)}) %collective-permute-start.68) | collective-permute-done | bytes 737312 | tf_op jit(solution)/shard_map/ppermute | solution.py:915
  (352 shorter events, 88.4 us)
Async XLA Ops:
  8.9 14.4 %collective-permute-start.23 = (bf16[592,384]{1,0:T(8,128)(2,1)}, bf16[592,384]{1,0:T(8,128)(2,1)S(1)}, u32[]{:S(2)}, u32[]{:S(2)}) collective-permute-start(bf16[592,384]{1,0:T(8,128)(2,1)} %get-tuple-element.121.b0), channel_id=1, source_target_pairs={{0,2},{1,3},{2,0},{3,1},{4,6},{5,7},{6,4},{7,5},{8,10},{9,11},{10,... | collective-permute-start | bytes 1363976 | tf_op jit(solution)/shard_map/ppermute | solution.py:680
  15.9 16.3 %collective-permute-start.1 = (bf16[592,384]{1,0:T(8,128)(2,1)}, bf16[592,384]{1,0:T(8,128)(2,1)S(1)}, u32[]{:S(2)}, u32[]{:S(2)}) collective-permute-start(bf16[592,384]{1,0:T(8,128)(2,1)} %get-tuple-element.109.b0), channel_id=1, source_target_pairs={{0,2},{1,3},{2,0},{3,1},{4,6},{5,7},{6,4},{7,5},{8,10},{9,11},{10,... | collective-permute-start | bytes 1363976 | tf_op jit(solution)/shard_map/ppermute | solution.py:680
  16.0 16.3 %collective-permute-start.22 = (bf16[592,384]{1,0:T(8,128)(2,1)}, bf16[592,384]{1,0:T(8,128)(2,1)S(1)}, u32[]{:S(2)}, u32[]{:S(2)}) collective-permute-start(bf16[592,384]{1,0:T(8,128)(2,1)} %get-tuple-element.121.b0), channel_id=1, source_target_pairs={{0,1},{1,0},{2,3},{3,2},{4,5},{5,4},{6,7},{7,6},{8,9},{9,8},{10,11... | collective-permute-start | bytes 1363976 | tf_op jit(solution)/shard_map/ppermute | solution.py:683
  23.3 8.9 %collective-permute-start.24 = (bf16[592,384]{1,0:T(8,128)(2,1)S(1)}, bf16[592,384]{1,0:T(8,128)(2,1)S(1)}, u32[]{:S(2)}, u32[]{:S(2)}) collective-permute-start(bf16[592,384]{1,0:T(8,128)(2,1)S(1)} %collective-permute-done.23.b2), channel_id=1, source_target_pairs={{0,1},{1,0},{2,3},{3,2},{4,5},{5,4},{6,7},{7,6},{8,9},{9,8},{10,11... | collective-permute-start | bytes 1363976 | tf_op jit(solution)/shard_map/ppermute | solution.py:683
  23.4 26.3 %collective-permute-start = (bf16[592,384]{1,0:T(8,128)(2,1)}, bf16[592,384]{1,0:T(8,128)(2,1)S(1)}, u32[]{:S(2)}, u32[]{:S(2)}) collective-permute-start(bf16[592,384]{1,0:T(8,128)(2,1)} %get-tuple-element.109.b0), channel_id=1, source_target_pairs={{0,1},{1,0},{2,3},{3,2},{4,5},{5,4},{6,7},{7,6},{8,9},{9,8},{10,11... | collective-permute-start | bytes 1363976 | tf_op jit(solution)/shard_map/ppermute | solution.py:683
  32.3 17.4 %collective-permute-start.2 = (bf16[592,384]{1,0:T(8,128)(2,1)S(1)}, bf16[592,384]{1,0:T(8,128)(2,1)S(1)}, u32[]{:S(2)}, u32[]{:S(2)}) collective-permute-start(bf16[592,384]{1,0:T(8,128)(2,1)S(1)} %collective-permute-done.1.b2), channel_id=1, source_target_pairs={{0,1},{1,0},{2,3},{3,2},{4,5},{5,4},{6,7},{7,6},{8,9},{9,8},{10,11... | collective-permute-start | bytes 1363976 | tf_op jit(solution)/shard_map/ppermute | solution.py:683
  47.8 17.7 %collective-permute-start.26 = (f32[8,128]{1,0:T(8,128)}, f32[8,128]{1,0:T(8,128)S(1)}, u32[]{:S(2)}, u32[]{:S(2)}) collective-permute-start(f32[8,128]{1,0:T(8,128)} %get-tuple-element.124.t0), channel_id=1, source_target_pairs={{0,2},{1,3},{2,0},{3,1},{4,6},{5,7},{6,4},{7,5},{8,10},{9,11},{10,... | collective-permute-start | bytes 12296 | tf_op jit(solution)/shard_map/ppermute | solution.py:680
  67.2 12.9 %collective-permute-start.3 = (f32[8,128]{1,0:T(8,128)}, f32[8,128]{1,0:T(8,128)S(1)}, u32[]{:S(2)}, u32[]{:S(2)}) collective-permute-start(f32[8,128]{1,0:T(8,128)} %get-tuple-element.112.t0), channel_id=1, source_target_pairs={{0,1},{1,0},{2,3},{3,2},{4,5},{5,4},{6,7},{7,6},{8,9},{9,8},{10,11... | collective-permute-start | bytes 12296 | tf_op jit(solution)/shard_map/ppermute | solution.py:683
  69.0 11.0 %collective-permute-start.5 = (f32[8,128]{1,0:T(8,128)S(1)}, f32[8,128]{1,0:T(8,128)S(1)}, u32[]{:S(2)}, u32[]{:S(2)}) collective-permute-start(f32[8,128]{1,0:T(8,128)S(1)} %collective-permute-done.4.t2), channel_id=1, source_target_pairs={{0,1},{1,0},{2,3},{3,2},{4,5},{5,4},{6,7},{7,6},{8,9},{9,8},{10,11... | collective-permute-start | bytes 12296 | tf_op jit(solution)/shard_map/ppermute | solution.py:683
  79.5 13.9 %collective-permute-start.28 = (bf16[2,576,384]{2,1,0:T(8,128)(2,1)}, bf16[2,576,384]{2,1,0:T(8,128)(2,1)S(1)}, u32[]{:S(2)}, u32[]{:S(2)}) collective-permute-start(bf16[2,576,384]{2,1,0:T(8,128)(2,1)} %get-tuple-element.126), channel_id=1, source_target_pairs={{0,1},{1,0},{2,3},{3,2},{4,5},{5,4},{6,7},{7,6},{8,9},{9,8},{10,11... | collective-permute-start | bytes 2654216 | tf_op jit(solution)/shard_map/ppermute | solution.py:683
  91.1 38.6 %collective-permute-start.18 = (bf16[2,576,384]{2,1,0:T(8,128)(2,1)S(1)}, bf16[2,576,384]{2,1,0:T(8,128)(2,1)S(1)}, u32[]{:S(2)}, u32[]{:S(2)}) collective-permute-start(bf16[2,576,384]{2,1,0:T(8,128)(2,1)S(1)} %copy-done.10), channel_id=1, source_target_pairs={{0,2},{1,3},{2,0},{3,1},{4,6},{5,7},{6,4},{7,5},{8,10},{9,11},{10,... | collective-permute-start | bytes 2654216 | tf_op jit(solution)/shard_map/ppermute | solution.py:680
  91.7 38.1 %collective-permute-start.12 = (bf16[2,80,384]{2,1,0:T(8,128)(2,1)S(1)}, bf16[2,80,384]{2,1,0:T(8,128)(2,1)S(1)}, u32[]{:S(2)}, u32[]{:S(2)}) collective-permute-start(bf16[2,80,384]{2,1,0:T(8,128)(2,1)S(1)} %pad.5.b0), channel_id=1, source_target_pairs={{0,2},{1,3},{2,0},{3,1},{4,6},{5,7},{6,4},{7,5},{8,10},{9,11},{10,... | collective-permute-start | bytes 368648 | tf_op jit(solution)/shard_map/ppermute | solution.py:680
  93.4 36.9 %collective-permute-start.11 = (bf16[2,80,384]{2,1,0:T(8,128)(2,1)S(1)}, bf16[2,80,384]{2,1,0:T(8,128)(2,1)S(1)}, u32[]{:S(2)}, u32[]{:S(2)}) collective-permute-start(bf16[2,80,384]{2,1,0:T(8,128)(2,1)S(1)} %pad.5.b0), channel_id=1, source_target_pairs={{0,1},{1,0},{2,3},{3,2},{4,5},{5,4},{6,7},{7,6},{8,9},{9,8},{10,11... | collective-permute-start | bytes 368648 | tf_op jit(solution)/shard_map/ppermute | solution.py:683
  96.4 29.4 %collective-permute-start.29 = (bf16[576,384]{1,0:T(8,128)(2,1)}, bf16[576,384]{1,0:T(8,128)(2,1)S(1)}, u32[]{:S(2)}, u32[]{:S(2)}) collective-permute-start(bf16[576,384]{1,0:T(8,128)(2,1)} %add_ffn_1.1), channel_id=1, source_target_pairs={{0,2},{1,3},{2,0},{3,1},{4,6},{5,7},{6,4},{7,5},{8,10},{9,11},{10,... | collective-permute-start | bytes 1327112 | tf_op jit(solution)/shard_map/ppermute | solution.py:680
  99.9 47.3 %collective-permute-start.7 = (bf16[576,384]{1,0:T(8,128)(2,1)}, bf16[576,384]{1,0:T(8,128)(2,1)S(1)}, u32[]{:S(2)}, u32[]{:S(2)}) collective-permute-start(bf16[576,384]{1,0:T(8,128)(2,1)} %add_ffn_0.1), channel_id=1, source_target_pairs={{0,2},{1,3},{2,0},{3,1},{4,6},{5,7},{6,4},{7,5},{8,10},{9,11},{10,... | collective-permute-start | bytes 1327112 | tf_op jit(solution)/shard_map/ppermute | solution.py:680
  129.4 22.1 %collective-permute-start.31 = (bf16[592,384]{1,0:T(8,128)(2,1)}, bf16[592,384]{1,0:T(8,128)(2,1)S(1)}, u32[]{:S(2)}, u32[]{:S(2)}) collective-permute-start(bf16[592,384]{1,0:T(8,128)(2,1)} %get-tuple-element.128.p0), channel_id=1, source_target_pairs={{0,2},{1,3},{2,0},{3,1},{4,6},{5,7},{6,4},{7,5},{8,10},{9,11},{10,... | collective-permute-start | bytes 1363976 | tf_op jit(solution)/shard_map/ppermute | solution.py:680
  129.8 23.1 %collective-permute-start.17 = (bf16[2,576,384]{2,1,0:T(8,128)(2,1)S(1)}, bf16[2,576,384]{2,1,0:T(8,128)(2,1)S(1)}, u32[]{:S(2)}, u32[]{:S(2)}) collective-permute-start(bf16[2,576,384]{2,1,0:T(8,128)(2,1)S(1)} %copy-done.10), channel_id=1, source_target_pairs={{0,1},{1,0},{2,3},{3,2},{4,5},{5,4},{6,7},{7,6},{8,9},{9,8},{10,11... | collective-permute-start | bytes 2654216 | tf_op jit(solution)/shard_map/ppermute | solution.py:683
  129.8 34.1 %collective-permute-start.19 = (bf16[2,576,384]{2,1,0:T(8,128)(2,1)S(1)}, bf16[2,576,384]{2,1,0:T(8,128)(2,1)S(1)}, u32[]{:S(2)}, u32[]{:S(2)}) collective-permute-start(bf16[2,576,384]{2,1,0:T(8,128)(2,1)S(1)} %collective-permute-done.18.g2), channel_id=1, source_target_pairs={{0,1},{1,0},{2,3},{3,2},{4,5},{5,4},{6,7},{7,6},{8,9},{9,8},{10,11... | collective-permute-start | bytes 2654216 | tf_op jit(solution)/shard_map/ppermute | solution.py:683
  137.9 9.3 %collective-permute-start.15 = (bf16[2,80,384]{2,1,0:T(8,128)(2,1)}, bf16[2,80,384]{2,1,0:T(8,128)(2,1)S(1)}, u32[]{:S(2)}, u32[]{:S(2)}) collective-permute-start(bf16[2,80,384]{2,1,0:T(8,128)(2,1)} %get-tuple-element.117.x0), channel_id=1, source_target_pairs={{0,2},{1,3},{2,0},{3,1},{4,6},{5,7},{6,4},{7,5},{8,10},{9,11},{10,... | collective-permute-start | bytes 368648 | tf_op jit(solution)/shard_map/ppermute | solution.py:680
  150.8 13.1 %collective-permute-start.9 = (bf16[592,384]{1,0:T(8,128)(2,1)}, bf16[592,384]{1,0:T(8,128)(2,1)S(1)}, u32[]{:S(2)}, u32[]{:S(2)}) collective-permute-start(bf16[592,384]{1,0:T(8,128)(2,1)} %get-tuple-element.116.p0), channel_id=1, source_target_pairs={{0,2},{1,3},{2,0},{3,1},{4,6},{5,7},{6,4},{7,5},{8,10},{9,11},{10,... | collective-permute-start | bytes 1363976 | tf_op jit(solution)/shard_map/ppermute | solution.py:680
  151.1 12.8 %collective-permute-start.30 = (bf16[592,384]{1,0:T(8,128)(2,1)S(1)}, bf16[592,384]{1,0:T(8,128)(2,1)S(1)}, u32[]{:S(2)}, u32[]{:S(2)}) collective-permute-start(bf16[592,384]{1,0:T(8,128)(2,1)S(1)} %copy-done.52), channel_id=1, source_target_pairs={{0,1},{1,0},{2,3},{3,2},{4,5},{5,4},{6,7},{7,6},{8,9},{9,8},{10,11... | collective-permute-start | bytes 1363976 | tf_op jit(solution)/shard_map/ppermute | solution.py:683
  151.4 12.5 %collective-permute-start.32 = (bf16[592,384]{1,0:T(8,128)(2,1)S(1)}, bf16[592,384]{1,0:T(8,128)(2,1)S(1)}, u32[]{:S(2)}, u32[]{:S(2)}) collective-permute-start(bf16[592,384]{1,0:T(8,128)(2,1)S(1)} %collective-permute-done.31.p2), channel_id=1, source_target_pairs={{0,1},{1,0},{2,3},{3,2},{4,5},{5,4},{6,7},{7,6},{8,9},{9,8},{10,11... | collective-permute-start | bytes 1363976 | tf_op jit(solution)/shard_map/ppermute | solution.py:683
  152.8 42.2 %collective-permute-start.8 = (bf16[592,384]{1,0:T(8,128)(2,1)}, bf16[592,384]{1,0:T(8,128)(2,1)S(1)}, u32[]{:S(2)}, u32[]{:S(2)}) collective-permute-start(bf16[592,384]{1,0:T(8,128)(2,1)} %get-tuple-element.116.p0), channel_id=1, source_target_pairs={{0,1},{1,0},{2,3},{3,2},{4,5},{5,4},{6,7},{7,6},{8,9},{9,8},{10,11... | collective-permute-start | bytes 1363976 | tf_op jit(solution)/shard_map/ppermute | solution.py:683
  163.9 31.2 %collective-permute-start.10 = (bf16[592,384]{1,0:T(8,128)(2,1)S(1)}, bf16[592,384]{1,0:T(8,128)(2,1)S(1)}, u32[]{:S(2)}, u32[]{:S(2)}) collective-permute-start(bf16[592,384]{1,0:T(8,128)(2,1)S(1)} %collective-permute-done.9.p2), channel_id=1, source_target_pairs={{0,1},{1,0},{2,3},{3,2},{4,5},{5,4},{6,7},{7,6},{8,9},{9,8},{10,11... | collective-permute-start | bytes 1363976 | tf_op jit(solution)/shard_map/ppermute | solution.py:683
  194.5 31.0 %collective-permute-start.45 = (bf16[2,672,384]{2,1,0:T(8,128)(2,1)}, bf16[2,672,384]{2,1,0:T(8,128)(2,1)S(1)}, u32[]{:S(2)}, u32[]{:S(2)}) collective-permute-start(bf16[2,672,384]{2,1,0:T(8,128)(2,1)} %get-tuple-element.148), channel_id=1, source_target_pairs={{0,1},{1,0},{2,3},{3,2},{4,5},{5,4},{6,7},{7,6},{8,9},{9,8},{10,11... | collective-permute-start | bytes 3096584 | tf_op jit(solution)/shard_map/ppermute | solution.py:683
  228.6 15.2 %collective-permute-start.46 = (bf16[672,384]{1,0:T(8,128)(2,1)}, bf16[672,384]{1,0:T(8,128)(2,1)S(1)}, u32[]{:S(2)}, u32[]{:S(2)}) collective-permute-start(bf16[672,384]{1,0:T(8,128)(2,1)} %add_ctx_1.1), channel_id=1, source_target_pairs={{0,2},{1,3},{2,0},{3,1},{4,6},{5,7},{6,4},{7,5},{8,10},{9,11},{10,... | collective-permute-start | bytes 1548296 | tf_op jit(solution)/shard_map/ppermute | solution.py:680
  232.0 22.4 %collective-permute-start.36 = (bf16[672,384]{1,0:T(8,128)(2,1)}, bf16[672,384]{1,0:T(8,128)(2,1)S(1)}, u32[]{:S(2)}, u32[]{:S(2)}) collective-permute-start(bf16[672,384]{1,0:T(8,128)(2,1)} %add_ctx_0.1), channel_id=1, source_target_pairs={{0,2},{1,3},{2,0},{3,1},{4,6},{5,7},{6,4},{7,5},{8,10},{9,11},{10,... | collective-permute-start | bytes 1548296 | tf_op jit(solution)/shard_map/ppermute | solution.py:680
  237.5 22.9 %collective-permute-start.33 = (bf16[2,576,384]{2,1,0:T(8,128)(2,1)}, bf16[2,576,384]{2,1,0:T(8,128)(2,1)S(1)}, u32[]{:S(2)}, u32[]{:S(2)}) collective-permute-start(bf16[2,576,384]{2,1,0:T(8,128)(2,1)} %get-tuple-element.131), channel_id=1, source_target_pairs={{0,1},{1,0},{2,3},{3,2},{4,5},{5,4},{6,7},{7,6},{8,9},{9,8},{10,11... | collective-permute-start | bytes 2654216 | tf_op jit(solution)/shard_map/ppermute | solution.py:683
  243.2 48.0 %collective-permute-start.20 = (bf16[2,576,384]{2,1,0:T(8,128)(2,1)}, bf16[2,576,384]{2,1,0:T(8,128)(2,1)S(1)}, u32[]{:S(2)}, u32[]{:S(2)}) collective-permute-start(bf16[2,576,384]{2,1,0:T(8,128)(2,1)} %get-tuple-element.120), channel_id=1, source_target_pairs={{0,1},{1,0},{2,3},{3,2},{4,5},{5,4},{6,7},{7,6},{8,9},{9,8},{10,11... | collective-permute-start | bytes 2654216 | tf_op jit(solution)/shard_map/ppermute | solution.py:683
  248.6 15.2 %collective-permute-start.48 = (bf16[576,384]{1,0:T(8,128)(2,1)}, bf16[576,384]{1,0:T(8,128)(2,1)S(1)}, u32[]{:S(2)}, u32[]{:S(2)}) collective-permute-start(bf16[576,384]{1,0:T(8,128)(2,1)} %get-tuple-element.150.b0), channel_id=1, source_target_pairs={{0,2},{1,3},{2,0},{3,1},{4,6},{5,7},{6,4},{7,5},{8,10},{9,11},{10,... | collective-permute-start | bytes 1327112 | tf_op jit(solution)/shard_map/ppermute | solution.py:680
  259.3 13.6 %collective-permute-start.38 = (bf16[576,384]{1,0:T(8,128)(2,1)}, bf16[576,384]{1,0:T(8,128)(2,1)S(1)}, u32[]{:S(2)}, u32[]{:S(2)}) collective-permute-start(bf16[576,384]{1,0:T(8,128)(2,1)} %get-tuple-element.135.b0), channel_id=1, source_target_pairs={{0,2},{1,3},{2,0},{3,1},{4,6},{5,7},{6,4},{7,5},{8,10},{9,11},{10,... | collective-permute-start | bytes 1327112 | tf_op jit(solution)/shard_map/ppermute | solution.py:680
  260.4 34.5 %collective-permute-start.47 = (bf16[576,384]{1,0:T(8,128)(2,1)S(1)}, bf16[576,384]{1,0:T(8,128)(2,1)S(1)}, u32[]{:S(2)}, u32[]{:S(2)}) collective-permute-start(bf16[576,384]{1,0:T(8,128)(2,1)S(1)} %copy-done.65), channel_id=1, source_target_pairs={{0,1},{1,0},{2,3},{3,2},{4,5},{5,4},{6,7},{7,6},{8,9},{9,8},{10,11... | collective-permute-start | bytes 1327112 | tf_op jit(solution)/shard_map/ppermute | solution.py:683
  260.4 48.2 %collective-permute-start.37 = (bf16[576,384]{1,0:T(8,128)(2,1)}, bf16[576,384]{1,0:T(8,128)(2,1)S(1)}, u32[]{:S(2)}, u32[]{:S(2)}) collective-permute-start(bf16[576,384]{1,0:T(8,128)(2,1)} %get-tuple-element.135.b0), channel_id=1, source_target_pairs={{0,1},{1,0},{2,3},{3,2},{4,5},{5,4},{6,7},{7,6},{8,9},{9,8},{10,11... | collective-permute-start | bytes 1327112 | tf_op jit(solution)/shard_map/ppermute | solution.py:683
  263.9 31.6 %collective-permute-start.49 = (bf16[576,384]{1,0:T(8,128)(2,1)S(1)}, bf16[576,384]{1,0:T(8,128)(2,1)S(1)}, u32[]{:S(2)}, u32[]{:S(2)}) collective-permute-start(bf16[576,384]{1,0:T(8,128)(2,1)S(1)} %collective-permute-done.48.b2), channel_id=1, source_target_pairs={{0,1},{1,0},{2,3},{3,2},{4,5},{5,4},{6,7},{7,6},{8,9},{9,8},{10,11... | collective-permute-start | bytes 1327112 | tf_op jit(solution)/shard_map/ppermute | solution.py:683
  272.9 35.7 %collective-permute-start.39 = (bf16[576,384]{1,0:T(8,128)(2,1)S(1)}, bf16[576,384]{1,0:T(8,128)(2,1)S(1)}, u32[]{:S(2)}, u32[]{:S(2)}) collective-permute-start(bf16[576,384]{1,0:T(8,128)(2,1)S(1)} %collective-permute-done.38.b2), channel_id=1, source_target_pairs={{0,1},{1,0},{2,3},{3,2},{4,5},{5,4},{6,7},{7,6},{8,9},{9,8},{10,11... | collective-permute-start | bytes 1327112 | tf_op jit(solution)/shard_map/ppermute | solution.py:683
  291.3 93.6 %collective-permute-start.69 = (bf16[4,192,1536]{2,1,0:T(8,128)(2,1)}, bf16[4,192,1536]{2,1,0:T(8,128)(2,1)S(1)}, u32[]{:S(2)}, u32[]{:S(2)}) collective-permute-start(bf16[4,192,1536]{2,1,0:T(8,128)(2,1)} %get-tuple-element.194), channel_id=1, source_target_pairs={{0,4},{4,0},{8,12},{12,8},{16,20},{20,16},{24,28},{28,24},{1,5},{5... | collective-permute-start | bytes 7077896 | tf_op jit(solution)/shard_map/ppermute | solution.py:908
  294.9 132.1 %collective-permute-start.34 = (bf16[576,384]{1,0:T(8,128)(2,1)S(1)}, bf16[576,384]{1,0:T(8,128)(2,1)S(1)}, u32[]{:S(2)}, u32[]{:S(2)}) collective-permute-start(bf16[576,384]{1,0:T(8,128)(2,1)S(1)} %copy-done.28), channel_id=1, source_target_pairs={{0,2},{1,3},{2,0},{3,1},{4,6},{5,7},{6,4},{7,5},{8,10},{9,11},{10,... | collective-permute-start | bytes 1327112 | tf_op jit(solution)/shard_map/ppermute | solution.py:680
  307.2 14.5 %collective-permute-start.51 = (f32[8,128]{1,0:T(8,128)}, f32[8,128]{1,0:T(8,128)S(1)}, u32[]{:S(2)}, u32[]{:S(2)}) collective-permute-start(f32[8,128]{1,0:T(8,128)} %get-tuple-element.154.c0), channel_id=1, source_target_pairs={{0,2},{1,3},{2,0},{3,1},{4,6},{5,7},{6,4},{7,5},{8,10},{9,11},{10,... | collective-permute-start | bytes 12296 | tf_op jit(solution)/shard_map/ppermute | solution.py:680
  308.6 28.5 %collective-permute-start.50 = (f32[8,128]{1,0:T(8,128)}, f32[8,128]{1,0:T(8,128)S(1)}, u32[]{:S(2)}, u32[]{:S(2)}) collective-permute-start(f32[8,128]{1,0:T(8,128)} %get-tuple-element.154.c0), channel_id=1, source_target_pairs={{0,1},{1,0},{2,3},{3,2},{4,5},{5,4},{6,7},{7,6},{8,9},{9,8},{10,11... | collective-permute-start | bytes 12296 | tf_op jit(solution)/shard_map/ppermute | solution.py:683
  320.9 17.6 %collective-permute-start.41 = (f32[8,128]{1,0:T(8,128)}, f32[8,128]{1,0:T(8,128)S(1)}, u32[]{:S(2)}, u32[]{:S(2)}) collective-permute-start(f32[8,128]{1,0:T(8,128)} %get-tuple-element.139.c0), channel_id=1, source_target_pairs={{0,2},{1,3},{2,0},{3,1},{4,6},{5,7},{6,4},{7,5},{8,10},{9,11},{10,... | collective-permute-start | bytes 12296 | tf_op jit(solution)/shard_map/ppermute | solution.py:680
  321.7 17.1 %collective-permute-start.52 = (f32[8,128]{1,0:T(8,128)S(1)}, f32[8,128]{1,0:T(8,128)S(1)}, u32[]{:S(2)}, u32[]{:S(2)}) collective-permute-start(f32[8,128]{1,0:T(8,128)S(1)} %collective-permute-done.51.c2), channel_id=1, source_target_pairs={{0,1},{1,0},{2,3},{3,2},{4,5},{5,4},{6,7},{7,6},{8,9},{9,8},{10,11... | collective-permute-start | bytes 12296 | tf_op jit(solution)/shard_map/ppermute | solution.py:683
  337.2 89.9 %collective-permute-start.21 = (bf16[576,384]{1,0:T(8,128)(2,1)S(1)}, bf16[576,384]{1,0:T(8,128)(2,1)S(1)}, u32[]{:S(2)}, u32[]{:S(2)}) collective-permute-start(bf16[576,384]{1,0:T(8,128)(2,1)S(1)} %copy-done.29), channel_id=1, source_target_pairs={{0,2},{1,3},{2,0},{3,1},{4,6},{5,7},{6,4},{7,5},{8,10},{9,11},{10,... | collective-permute-start | bytes 1327112 | tf_op jit(solution)/shard_map/ppermute | solution.py:680
  338.6 14.1 %collective-permute-start.40 = (f32[8,128]{1,0:T(8,128)S(1)}, f32[8,128]{1,0:T(8,128)S(1)}, u32[]{:S(2)}, u32[]{:S(2)}) collective-permute-start(f32[8,128]{1,0:T(8,128)S(1)} %copy-done.82), channel_id=1, source_target_pairs={{0,1},{1,0},{2,3},{3,2},{4,5},{5,4},{6,7},{7,6},{8,9},{9,8},{10,11... | collective-permute-start | bytes 12296 | tf_op jit(solution)/shard_map/ppermute | solution.py:683
  338.8 14.8 %collective-permute-start.42 = (f32[8,128]{1,0:T(8,128)S(1)}, f32[8,128]{1,0:T(8,128)S(1)}, u32[]{:S(2)}, u32[]{:S(2)}) collective-permute-start(f32[8,128]{1,0:T(8,128)S(1)} %collective-permute-done.41.c2), channel_id=1, source_target_pairs={{0,1},{1,0},{2,3},{3,2},{4,5},{5,4},{6,7},{7,6},{8,9},{9,8},{10,11... | collective-permute-start | bytes 12296 | tf_op jit(solution)/shard_map/ppermute | solution.py:683
  352.7 165.7 %collective-permute-start.65 = (bf16[4,192,1920]{2,1,0:T(8,128)(2,1)}, bf16[4,192,1920]{2,1,0:T(8,128)(2,1)}, u32[]{:S(2)}, u32[]{:S(2)}) collective-permute-start(bf16[4,192,1920]{2,1,0:T(8,128)(2,1)} %get-tuple-element.186), channel_id=1, source_target_pairs={{0,4},{4,0},{8,12},{12,8},{16,20},{20,16},{24,28},{28,24},{1,5},{5... | collective-permute-start | bytes 8847368 | tf_op jit(solution)/shard_map/ppermute | solution.py:908
  369.1 55.3 %collective-permute-start.62 = (f32[144,384]{1,0:T(8,128)}, f32[144,384]{1,0:T(8,128)S(1)}, u32[]{:S(2)}, u32[]{:S(2)}) collective-permute-start(f32[144,384]{1,0:T(8,128)} %pack_early.1), channel_id=1, source_target_pairs={{0,4},{4,0},{8,12},{12,8},{16,20},{20,16},{24,28},{28,24},{1,5},{5... | collective-permute-start | bytes 663560 | tf_op jit(solution)/shard_map/ppermute | solution.py:923
  384.9 128.4 %collective-permute-start.58 = (bf16[4,192,1536]{2,1,0:T(8,128)(2,1)}, bf16[4,192,1536]{2,1,0:T(8,128)(2,1)}, u32[]{:S(2)}, u32[]{:S(2)}) collective-permute-start(bf16[4,192,1536]{2,1,0:T(8,128)(2,1)} %get-tuple-element.169), channel_id=1, source_target_pairs={{0,4},{4,0},{8,12},{12,8},{16,20},{20,16},{24,28},{28,24},{1,5},{5... | collective-permute-start | bytes 7077896 | tf_op jit(solution)/shard_map/ppermute | solution.py:908
  424.4 24.8 %collective-permute-start.70 = (bf16[192,1536]{1,0:T(8,128)(2,1)S(1)}, bf16[192,1536]{1,0:T(8,128)(2,1)S(1)}, u32[]{:S(2)}, u32[]{:S(2)}) collective-permute-start(bf16[192,1536]{1,0:T(8,128)(2,1)S(1)} %fusion.8), channel_id=1, source_target_pairs={{0,16},{4,20},{16,24},{20,28},{24,8},{28,12},{8,0},{12,4},{1,17},{... | collective-permute-start | bytes 1769480 | tf_op jit(solution)/shard_map/ppermute | solution.py:915
  427.0 16.4 %collective-permute-start.63 = (f32[144,384]{1,0:T(8,128)S(1)}, f32[144,384]{1,0:T(8,128)S(1)}, u32[]{:S(2)}, u32[]{:S(2)}) collective-permute-start(f32[144,384]{1,0:T(8,128)S(1)} %add.158), channel_id=1, source_target_pairs={{0,8},{4,12},{8,0},{12,4},{16,24},{20,28},{24,16},{28,20},{1,9},{5... | collective-permute-start | bytes 663560 | tf_op jit(solution)/shard_map/ppermute | solution.py:923
  427.1 36.9 %collective-permute-start.53 = (bf16[2,592,384]{2,1,0:T(8,128)(2,1)}, bf16[2,592,384]{2,1,0:T(8,128)(2,1)S(1)}, u32[]{:S(2)}, u32[]{:S(2)}) collective-permute-start(bf16[2,592,384]{2,1,0:T(8,128)(2,1)} %get-tuple-element.157), channel_id=1, source_target_pairs={{0,1},{1,0},{2,3},{3,2},{4,5},{5,4},{6,7},{7,6},{8,9},{9,8},{10,11... | collective-permute-start | bytes 2727944 | tf_op jit(solution)/shard_map/ppermute | solution.py:683
  443.4 24.2 %collective-permute-start.43 = (bf16[2,592,384]{2,1,0:T(8,128)(2,1)}, bf16[2,592,384]{2,1,0:T(8,128)(2,1)S(1)}, u32[]{:S(2)}, u32[]{:S(2)}) collective-permute-start(bf16[2,592,384]{2,1,0:T(8,128)(2,1)} %get-tuple-element.142), channel_id=1, source_target_pairs={{0,1},{1,0},{2,3},{3,2},{4,5},{5,4},{6,7},{7,6},{8,9},{9,8},{10,11... | collective-permute-start | bytes 2727944 | tf_op jit(solution)/shard_map/ppermute | solution.py:683
  449.2 13.5 %collective-permute-start.64 = (f32[144,384]{1,0:T(8,128)S(1)}, f32[144,384]{1,0:T(8,128)S(1)}, u32[]{:S(2)}, u32[]{:S(2)}) collective-permute-start(f32[144,384]{1,0:T(8,128)S(1)} %add.159), channel_id=1, source_target_pairs={{0,16},{4,20},{8,24},{12,28},{16,0},{20,4},{24,8},{28,12},{1,17},{... | collective-permute-start | bytes 663560 | tf_op jit(solution)/shard_map/ppermute | solution.py:923
  462.8 47.3 %collective-permute-start.71 = (bf16[192,1536]{1,0:T(8,128)(2,1)S(1)}, bf16[192,1536]{1,0:T(8,128)(2,1)}, u32[]{:S(2)}, u32[]{:S(2)}) collective-permute-start(bf16[192,1536]{1,0:T(8,128)(2,1)S(1)} %fusion.2), channel_id=1, source_target_pairs={{0,16},{4,20},{16,24},{20,28},{24,8},{28,12},{8,0},{12,4},{1,17},{... | collective-permute-start | bytes 1769480 | tf_op jit(solution)/shard_map/ppermute | solution.py:915
  467.0 13.5 %collective-permute-start.54 = (bf16[592,384]{1,0:T(8,128)(2,1)}, bf16[592,384]{1,0:T(8,128)(2,1)S(1)}, u32[]{:S(2)}, u32[]{:S(2)}) collective-permute-start(bf16[592,384]{1,0:T(8,128)(2,1)} %add_in_1.1), channel_id=1, source_target_pairs={{0,2},{1,3},{2,0},{3,1},{4,6},{5,7},{6,4},{7,5},{8,10},{9,11},{10,... | collective-permute-start | bytes 1363976 | tf_op jit(solution)/shard_map/ppermute | solution.py:680
  470.7 19.0 %collective-permute-start.44 = (bf16[592,384]{1,0:T(8,128)(2,1)}, bf16[592,384]{1,0:T(8,128)(2,1)S(1)}, u32[]{:S(2)}, u32[]{:S(2)}) collective-permute-start(bf16[592,384]{1,0:T(8,128)(2,1)} %add_in_0.1), channel_id=1, source_target_pairs={{0,2},{1,3},{2,0},{3,1},{4,6},{5,7},{6,4},{7,5},{8,10},{9,11},{10,... | collective-permute-start | bytes 1363976 | tf_op jit(solution)/shard_map/ppermute | solution.py:680
  504.5 8.7 %collective-permute-start.56 = (f32[16,384]{1,0:T(8,128)S(1)}, f32[16,384]{1,0:T(8,128)S(1)}, u32[]{:S(2)}, u32[]{:S(2)}) collective-permute-start(f32[16,384]{1,0:T(8,128)S(1)} %add.144), channel_id=1, source_target_pairs={{0,8},{4,12},{8,0},{12,4},{16,24},{20,28},{24,16},{28,20},{1,9},{5... | collective-permute-start | bytes 73736 | tf_op jit(solution)/shard_map/ppermute | solution.py:923
  512.7 52.2 %collective-permute-start.72 = (bf16[192,1536]{1,0:T(8,128)(2,1)}, bf16[192,1536]{1,0:T(8,128)(2,1)}, u32[]{:S(2)}, u32[]{:S(2)}) collective-permute-start(bf16[192,1536]{1,0:T(8,128)(2,1)} %fusion.3), channel_id=1, source_target_pairs={{0,16},{4,20},{16,24},{20,28},{24,8},{28,12},{8,0},{12,4},{1,17},{... | collective-permute-start | bytes 1769480 | tf_op jit(solution)/shard_map/ppermute | solution.py:915
  513.2 47.1 %collective-permute-start.57 = (f32[16,384]{1,0:T(8,128)S(1)}, f32[16,384]{1,0:T(8,128)S(1)}, u32[]{:S(2)}, u32[]{:S(2)}) collective-permute-start(f32[16,384]{1,0:T(8,128)S(1)} %add.145), channel_id=1, source_target_pairs={{0,16},{4,20},{8,24},{12,28},{16,0},{20,4},{24,8},{28,12},{1,17},{... | collective-permute-start | bytes 73736 | tf_op jit(solution)/shard_map/ppermute | solution.py:923
  515.5 46.0 %collective-permute-start.59 = (bf16[192,1536]{1,0:T(8,128)(2,1)}, bf16[192,1536]{1,0:T(8,128)(2,1)}, u32[]{:S(2)}, u32[]{:S(2)}) collective-permute-start(bf16[192,1536]{1,0:T(8,128)(2,1)} %fusion.7), channel_id=1, source_target_pairs={{0,16},{4,20},{16,24},{20,28},{24,8},{28,12},{8,0},{12,4},{1,17},{... | collective-permute-start | bytes 1769480 | tf_op jit(solution)/shard_map/ppermute | solution.py:915
  520.6 42.7 %collective-permute-start.66 = (bf16[192,1920]{1,0:T(8,128)(2,1)}, bf16[192,1920]{1,0:T(8,128)(2,1)}, u32[]{:S(2)}, u32[]{:S(2)}) collective-permute-start(bf16[192,1920]{1,0:T(8,128)(2,1)} %fusion.6), channel_id=1, source_target_pairs={{0,16},{4,20},{16,24},{20,28},{24,8},{28,12},{8,0},{12,4},{1,17},{... | collective-permute-start | bytes 2211848 | tf_op jit(solution)/shard_map/ppermute | solution.py:915
  563.2 16.2 %collective-permute-start.60 = (bf16[192,1536]{1,0:T(8,128)(2,1)S(1)}, bf16[192,1536]{1,0:T(8,128)(2,1)S(1)}, u32[]{:S(2)}, u32[]{:S(2)}) collective-permute-start(bf16[192,1536]{1,0:T(8,128)(2,1)S(1)} %fusion.4), channel_id=1, source_target_pairs={{0,16},{4,20},{16,24},{20,28},{24,8},{28,12},{8,0},{12,4},{1,17},{... | collective-permute-start | bytes 1769480 | tf_op jit(solution)/shard_map/ppermute | solution.py:915
  564.9 30.3 %collective-permute-start.67 = (bf16[192,1920]{1,0:T(8,128)(2,1)S(1)}, bf16[192,1920]{1,0:T(8,128)(2,1)S(1)}, u32[]{:S(2)}, u32[]{:S(2)}) collective-permute-start(bf16[192,1920]{1,0:T(8,128)(2,1)S(1)} %fusion), channel_id=1, source_target_pairs={{0,16},{4,20},{16,24},{20,28},{24,8},{28,12},{8,0},{12,4},{1,17},{... | collective-permute-start | bytes 2211848 | tf_op jit(solution)/shard_map/ppermute | solution.py:915
  580.7 27.2 %collective-permute-start.61 = (bf16[192,1536]{1,0:T(8,128)(2,1)S(1)}, bf16[192,1536]{1,0:T(8,128)(2,1)S(1)}, u32[]{:S(2)}, u32[]{:S(2)}) collective-permute-start(bf16[192,1536]{1,0:T(8,128)(2,1)S(1)} %fusion.5), channel_id=1, source_target_pairs={{0,16},{4,20},{16,24},{20,28},{24,8},{28,12},{8,0},{12,4},{1,17},{... | collective-permute-start | bytes 1769480 | tf_op jit(solution)/shard_map/ppermute | solution.py:915
  596.6 26.1 %collective-permute-start.68 = (bf16[192,1920]{1,0:T(8,128)(2,1)S(1)}, bf16[192,1920]{1,0:T(8,128)(2,1)S(1)}, u32[]{:S(2)}, u32[]{:S(2)}) collective-permute-start(bf16[192,1920]{1,0:T(8,128)(2,1)S(1)} %fusion.1), channel_id=1, source_target_pairs={{0,16},{4,20},{16,24},{20,28},{24,8},{28,12},{8,0},{12,4},{1,17},{... | collective-permute-start | bytes 2211848 | tf_op jit(solution)/shard_map/ppermute | solution.py:915
  (98 other events, 1007.9 us)
